TPU v7x, 512 devices: a whole 4x8x8 slice. The times are simulated.
512 devices in a mesh: pages: 64 (over y, x, core), heads: 8 (over z).
Axes of the slice: x: 4, y: 8, z: 8, core: 2. Of those that a mesh axis runs over, the one named last changes fastest.
Arguments:
- prefill_latent: bfloat16 [512, 64, 576], P('pages'), may hold values from -6 to 6
- stretch_page: int32 [512], replicated, may hold values from 0 to 511, as said below
- page_table: int32 [512, 2], replicated, may hold values from 0 to 63, as said below
- page_list: int32 [64, 64], replicated, may hold values from 0 to 511, as said below
- lengths: int32 [64], replicated, may hold values from 64 to 4096, as said below
- queries: bfloat16 [2, 64, 2, 128, 576], P(None, 'pages', None, 'heads'), may hold values from -64 to 64
- new_latent: bfloat16 [2, 64, 2, 576], P(None, 'pages'), may hold values from -24 to 24
Outputs:
- attended: bfloat16 [2, 64, 2, 128, 512], P(None, 'pages', None, 'heads')
- cache_pool: bfloat16 [512, 64, 576], P('pages', 'heads')
Inputs may be any that keep to these rules, and one draw needn't show every extreme that they name: `page_table`: page j lies on owner (j + a) mod 64 for one a of each draw; each owner's 8 slots hold different pages. `stretch_page`: stretches d * 8 to (d + 1) * 8 - 1 name two runs of half of 8 consecutive logical pages, runs b and 127 - b for a b of their own; every logical page once. `page_list`: each row names 64 consecutive logical pages. `lengths`: some request reads all of its list.
All inputs are finite; a program needn't handle non-finite values.
Results may differ from a plain program's by a relative error of at most 0.0022.
Values may be sent and summed in bfloat16 or wider, within the bound.
A program may use at most 64 MiB of HBM per device.

v0:
```python
import math

import jax
import jax.numpy as jnp
from jax import lax
from jax.sharding import PartitionSpec as P

LAT = 512


SOFTMAX_SCALE = 192.0 ** (-0.5)
MASKED_SCORE = -1e30


def owner_ranks(owners):
    stretch_count = owners.shape[-1]
    stretch_order = jnp.arange(stretch_count, dtype=jnp.int32)
    same_owner = owners[:, :, None] == owners[:, None, :]
    earlier = stretch_order[None, None, :] < stretch_order[None, :, None]
    return jnp.sum(jnp.logical_and(same_owner, earlier), axis=-1)


def push_cache(prefill_latent, stretch_page, page_table):
    groups = lax.axis_size("pages")
    device_index = lax.axis_index("pages")
    slot_count = prefill_latent.shape[0]
    row_share = prefill_latent.shape[1] // lax.axis_size("heads")
    capacity = max(1, slot_count // groups)
    head_index = lax.axis_index("heads")
    share = lax.dynamic_slice_in_dim(prefill_latent, head_index * row_share, row_share, 1)
    owners = page_table[stretch_page, 0].reshape(groups, slot_count)
    places = page_table[stretch_page, 1].reshape(groups, slot_count)
    stretch_rank = owner_ranks(owners)
    own_owner = lax.dynamic_index_in_dim(owners, device_index, 0, keepdims=False)
    own_rank = lax.dynamic_index_in_dim(stretch_rank, device_index, 0, keepdims=False)
    target = own_owner * capacity + own_rank
    outgoing = jnp.zeros((groups * capacity,) + share.shape[1:], share.dtype).at[target].set(share)
    outgoing = outgoing.reshape((groups, capacity) + share.shape[1:])
    incoming = lax.all_to_all(outgoing, "pages", split_axis=0, concat_axis=0, tiled=True)
    source = jnp.arange(groups, dtype=jnp.int32)[:, None]
    arrival = jnp.where(owners == device_index, source * capacity + stretch_rank, groups * capacity)
    slot_of = jnp.full((groups * capacity + 1,), slot_count, jnp.int32)
    slot_of = slot_of.at[arrival.reshape(-1)].set(places.reshape(-1))
    cache_part = jnp.zeros((slot_count,) + share.shape[1:], share.dtype)
    cache_part = cache_part.at[slot_of[:-1]].set(
        incoming.reshape((groups * capacity,) + share.shape[1:]), mode="drop"
    )
    return (lax.all_gather(cache_part, "heads", axis=1, tiled=True), cache_part)


def merge_blocks(stacked_part):
    moved = jnp.moveaxis(stacked_part, 0, 1)
    return moved.reshape((moved.shape[0], moved.shape[1] * moved.shape[2]) + moved.shape[3:])


def make_compute(cache_pool, page_table, page_list, lengths, device_index, groups):
    per_owner = page_list.shape[1] // groups
    page_rows = cache_pool.shape[1]

    def block_terms(query_block, first_row):
        block_size = query_block.shape[1]
        list_rows = lax.dynamic_slice_in_dim(page_list, first_row, block_size, 0)
        token_spans = lax.dynamic_slice_in_dim(lengths, first_row, block_size, 0)
        first_owner = page_table[list_rows[:, 0], 0]
        offset = jnp.mod(device_index - first_owner, groups)
        positions = offset[:, None] + groups * jnp.arange(per_owner, dtype=jnp.int32)[None, :]
        page_ids = jnp.take_along_axis(list_rows, positions, axis=1)
        cached = cache_pool[page_table[page_ids, 1]]
        token_index = jnp.arange(page_rows, dtype=jnp.int32)
        is_live = (
            positions[:, :, None] * page_rows + token_index[None, None, :]
            < token_spans[:, None, None]
        )
        scores = (
            jnp.einsum(
                "snrhc,nitc->snrhit", query_block, cached, preferred_element_type=jnp.float32
            )
            * SOFTMAX_SCALE
        )
        live_mask = is_live[None, :, None, None]
        peak_score = jnp.max(jnp.where(live_mask, scores, MASKED_SCORE), axis=(4, 5))
        weights = jnp.where(live_mask, jnp.exp(scores - peak_score[..., None, None]), 0.0)
        weight_sum = jnp.sum(weights, axis=(4, 5))
        summed = jnp.einsum(
            "snrhit,nitc->snrhc",
            weights.astype(jnp.bfloat16),
            cached[..., :LAT],
            preferred_element_type=jnp.float32,
        )
        return (summed, peak_score, weight_sum)

    def compute(query_piece, first_row):
        request_count = query_piece.shape[1]
        group_size = math.gcd(request_count, 8)
        block_count = request_count // group_size

        def one_block(block_index):
            block_start = block_index * group_size
            query_block = lax.dynamic_slice_in_dim(query_piece, block_start, group_size, 1)
            return block_terms(query_block, block_start)

        results = lax.map(one_block, jnp.arange(block_count, dtype=jnp.int32))
        return tuple((merge_blocks(stacked_part) for stacked_part in results))

    return compute


def fresh_terms(queries, new_latent):
    step_count, request_count, row_count = new_latent.shape[:3]
    fresh_keys = jnp.transpose(new_latent, (1, 0, 2, 3)).reshape(
        request_count, step_count * row_count, new_latent.shape[3]
    )
    scores = (
        jnp.einsum("snrhc,nmc->snrhm", queries, fresh_keys, preferred_element_type=jnp.float32)
        * SOFTMAX_SCALE
    )
    order_index = jnp.arange(step_count * row_count, dtype=jnp.int32)
    visible = (order_index[None, :] <= order_index[:, None]).reshape(
        step_count, row_count, step_count * row_count
    )
    visible = visible[:, None, :, None, :]
    peak_score = jnp.max(jnp.where(visible, scores, MASKED_SCORE), axis=-1)
    weights = jnp.where(visible, jnp.exp(scores - peak_score[..., None]), 0.0)
    weight_sum = jnp.sum(weights, axis=-1)
    summed = jnp.einsum(
        "snrhm,nmc->snrhc",
        weights.astype(jnp.bfloat16),
        fresh_keys[..., :LAT],
        preferred_element_type=jnp.float32,
    )
    return (summed, peak_score, weight_sum)


def combine(arrived, local_terms):
    summed, peak_score, weight_sum = arrived
    own_sum, own_peak, own_total = local_terms
    top_score = jnp.maximum(jnp.max(peak_score, axis=0), own_peak)
    rescale = jnp.exp(peak_score - top_score[None])
    own_scale = jnp.exp(own_peak - top_score)
    denominator = jnp.sum(rescale * weight_sum, axis=0) + own_scale * own_total
    numerator = jnp.sum(rescale[..., None] * summed, axis=0) + own_scale[..., None] * own_sum
    return (numerator / denominator[..., None]).astype(jnp.bfloat16)


def local(prefill_latent, stretch_page, page_table, page_list, lengths, queries, new_latent):
    groups = lax.axis_size("pages")
    device_index = lax.axis_index("pages")
    cache_pool, owned_rows = push_cache(prefill_latent, stretch_page, page_table)
    compute = make_compute(cache_pool, page_table, page_list, lengths, device_index, groups)
    local_terms = fresh_terms(queries, new_latent)
    results = []
    for step_index in range(queries.shape[0]):
        summed, peak_score, weight_sum = compute(
            lax.all_gather(queries[step_index : step_index + 1], "pages", axis=1, tiled=True),
            jnp.int32(0),
        )
        arrived = (
            lax.all_to_all(summed[None], "pages", split_axis=2, concat_axis=0, tiled=True),
            lax.all_to_all(peak_score[None], "pages", split_axis=2, concat_axis=0, tiled=True),
            lax.all_to_all(weight_sum[None], "pages", split_axis=2, concat_axis=0, tiled=True),
        )
        step_terms = tuple((term[step_index : step_index + 1] for term in local_terms))
        results.append(combine(arrived, step_terms))
    attended = jnp.concatenate(results, axis=0)
    return (attended, owned_rows)


def solution(mesh):
    in_specs = (
        P("pages", None, None),
        P(),
        P(),
        P(),
        P(),
        P(None, "pages", None, "heads", None),
        P(None, "pages", None, None),
    )
    out_specs = (P(None, "pages", None, "heads", None), P("pages", "heads", None))
    return jax.shard_map(local, mesh=mesh, in_specs=in_specs, out_specs=out_specs, check_vma=False)
```

profile of v0, /device:TPU:1, one launch (start us, length us, event | category | flops | bytes accessed | tf_op | source)
XLA Modules:
  0.0 503.3 jit_solution(8778389799785882696)
XLA Ops:
  7.2 1.5 fusion.72
  9.4 4.9 gather_fusion.8
  15.8 2.0 scatter_fusion
  17.8 11.6 %all-to-all-start = ((bf16[64,1,8,576]{3,2,1,0:T(8,128)(2,1)}), bf16[64,1,8,576]{3,2,1,0:T(8,128)(2,1)S(1)}, u32[]{:S(2)}, u32[]{:S(2)}) async-start(bf16[64,1,8,576]{3,2,1,0:T(8,128)(2,1)} %bitcast.57), calls=%async_computation | async-start | bytes 1310720 | tf_op jit(solution)/shard_map/all_to_all | solution.py:39
  30.4 4.8 gather_fusion.9
  35.4 2.4 scatter_custom_fusion
  37.8 12.9 %all-to-all-done = bf16[64,1,8,576]{3,2,1,0:T(8,128)(2,1)S(1)} async-done(((bf16[64,1,8,576]{3,2,1,0:T(8,128)(2,1)}), bf16[64,1,8,576]{3,2,1,0:T(8,128)(2,1)S(1)}, u32[]{:S(2)}, u32[]{:S(2)}) %all-to-all-start) | async-done | bytes 589856 | tf_op jit(solution)/shard_map/all_to_all | solution.py:39
  50.7 2.7 scatter_fusion.1
  53.4 26.2 %all_gather.9 = bf16[8,64,576]{2,1,0:T(8,128)(2,1)S(1)} all-gather(bf16[8,8,576]{2,1,0:T(8,128)(2,1)S(1)} %scatter_fusion.1), channel_id=1, replica_groups=mesh['pages'=64,'heads'=8] {'heads'}, dimensions={1}, use_global_device_ids=true | all-gather | bytes 663552 | tf_op jit(solution)/shard_map/all_gather | solution.py:48
  79.6 22.8 %all-gather.3.cloned.1.call-done = bf16[1,64,2,16,576]{4,3,2,0,1:T(8,128)(2,1)} async-done(((bf16[1,1,2,16,576]{4,3,2,0,1:T(8,128)(2,1)}), bf16[1,64,2,16,576]{4,3,2,0,1:T(8,128)(2,1)}) %all-gather.3.cloned.1.call-update) | async-done | bytes 2359312 | tf_op jit(solution)/shard_map/all_gather | solution.py:154
  102.4 2.5 broadcast.595.clone
  105.6 62.1 %while.32 = (s32[]{:T(128)}, f32[8,1,8,2,16,512]{5,4,3,2,1,0:T(8,128)}, f32[8,1,8,2,16]{4,3,2,1,0:T(2,128)}, f32[8,1,8,2,16]{4,3,2,1,0:T(2,128)S(1)}, s32[8]{0:T...) while((s32[]{:T(128)}, ...), condition=%wide.region_7.9_spmd, body=%wide.region_4.0_spmd.sunk | while | flops 35801140 | bytes 3465283 | solution.py:102
  117.8 1.4 select_reduce_fusion.5
  133.3 1.4 select_reduce_fusion.5
  141.1 1.4 select_reduce_fusion.5
  148.9 1.4 select_reduce_fusion.5
  156.6 1.4 select_reduce_fusion.5
  164.4 1.4 select_reduce_fusion.5
  167.7 6.6 %all-to-all-start.1 = ((f32[1,1,64,2,16]{4,3,1,0,2:T(2,128)}), f32[1,1,64,2,16]{4,3,1,0,2:T(2,128)S(1)}, u32[]{:S(2)}, u32[]{:S(2)}) async-start(f32[1,1,64,2,16]{4,3,1,0,2:T(2,128)} %bitcast.61), calls=%async_computation.1 | async-start | bytes 131072 | tf_op jit(solution)/shard_map/all_to_all | solution.py:159
  174.3 12.5 %all-gather.5.cloned.1.call-done = bf16[1,64,2,16,576]{4,3,2,0,1:T(8,128)(2,1)} async-done(((bf16[1,1,2,16,576]{4,3,2,0,1:T(8,128)(2,1)}), bf16[1,64,2,16,576]{4,3,2,0,1:T(8,128)(2,1)}) %all-gather.5.cloned.1.call-update) | async-done | bytes 2359312 | tf_op jit(solution)/shard_map/all_gather | solution.py:154
  186.7 2.5 broadcast.595.clone.1
  189.3 57.3 %while.33 = (s32[]{:T(128)}, f32[8,1,8,2,16,512]{5,4,3,2,1,0:T(8,128)}, f32[8,1,8,2,16]{4,3,2,1,0:T(2,128)S(1)}, f32[8,1,8,2,16]{4,3,2,1,0:T(2,128)S(1)}, s32[8]...) while((s32[]{:T(128)}, ...), condition=%wide.region_16.18_spmd, body=%wide.region_13.17_spmd.sunk | while | flops 35801140 | bytes 3464775 | solution.py:102
  208.1 1.4 select_reduce_fusion.6
  215.2 1.4 select_reduce_fusion.6
  246.6 16.8 %all_to_all.83 = f32[1,1,64,2,16]{4,3,1,0,2:T(2,128)S(1)} all-to-all(f32[1,1,64,2,16]{4,3,1,0,2:T(2,128)S(1)} %bitcast.358), channel_id=1, replica_groups=mesh['pages'=64,'heads'=8] {'pages'}, dimensions={2} | all-to-all | bytes 16384 | tf_op jit(solution)/shard_map/all_to_all | solution.py:159
  263.4 13.7 %all_to_all.84 = f32[1,1,64,2,16]{4,3,1,0,2:T(2,128)S(1)} all-to-all(f32[1,1,64,2,16]{4,3,1,0,2:T(2,128)S(1)} %bitcast.359), channel_id=1, replica_groups=mesh['pages'=64,'heads'=8] {'pages'}, dimensions={2} | all-to-all | bytes 16384 | tf_op jit(solution)/shard_map/all_to_all | solution.py:160
  277.1 13.7 %all_to_all.85 = f32[1,1,64,2,16]{4,3,1,0,2:T(2,128)S(1)} all-to-all(f32[1,1,64,2,16]{4,3,1,0,2:T(2,128)S(1)} %bitcast.360), channel_id=1, replica_groups=mesh['pages'=64,'heads'=8] {'pages'}, dimensions={2} | all-to-all | bytes 16384 | tf_op jit(solution)/shard_map/all_to_all | solution.py:160
  290.9 100.2 %all_to_all.86 = f32[1,1,64,2,16,512]{5,4,3,1,0,2:T(8,128)} all-to-all(f32[1,1,64,2,16,512]{5,4,3,1,0,2:T(8,128)} %bitcast.353), channel_id=1, replica_groups=mesh['pages'=64,'heads'=8] {'pages'}, dimensions={2} | all-to-all | bytes 8388608 | tf_op jit(solution)/shard_map/all_to_all | solution.py:158
  391.1 7.4 %all-to-all-start.2 = ((f32[1,1,64,2,16,512]{5,4,3,1,0,2:T(8,128)}), f32[1,1,64,2,16,512]{5,4,3,1,0,2:T(8,128)}, u32[]{:S(2)}, u32[]{:S(2)}) async-start(f32[1,1,64,2,16,512]{5,4,3,1,0,2:T(8,128)} %bitcast.354), calls=%async_computation.2 | async-start | bytes 8388608 | tf_op jit(solution)/shard_map/all_to_all | solution.py:158
  399.7 2.6 fusion.36
  402.3 90.8 %all-to-all-done.2 = f32[1,1,64,2,16,512]{5,4,3,1,0,2:T(8,128)} async-done(((f32[1,1,64,2,16,512]{5,4,3,1,0,2:T(8,128)}), f32[1,1,64,2,16,512]{5,4,3,1,0,2:T(8,128)}, u32[]{:S(2)}, u32[]{:S(2)}) %all-to-all-start.2) | async-done | bytes 4194336 | tf_op jit(solution)/shard_map/all_to_all | solution.py:158
  493.1 2.6 fusion.37
  (418 shorter events, 101.7 us)
Async XLA Ops:
  7.2 7.7 %copy-start = (bf16[8,64,576]{2,1,0:T(8,128)(2,1)S(1)}, bf16[8,64,576]{2,1,0:T(8,128)(2,1)}, u32[]{:S(2)}) copy-start(bf16[8,64,576]{2,1,0:T(8,128)(2,1)} %param.13) | copy-start | bytes 1769476
  7.2 23.2 %copy-start.1 = (s32[512,2]{0,1:T(2,128)S(1)}, s32[512,2]{0,1:T(2,128)}, u32[]{:S(2)}) copy-start(s32[512,2]{0,1:T(2,128)} %param.15) | copy-start | bytes 12292
  7.2 28.1 %copy-start.4 = (s32[64,64]{1,0:T(8,128)S(1)}, s32[64,64]{1,0:T(8,128)}, u32[]{:S(2)}) copy-start(s32[64,64]{1,0:T(8,128)} %param.16) | copy-start | bytes 49156
  7.2 95.2 %all-gather.3.cloned.1.call-start = ((), (), s32[]{:S(2)}) async-start(), calls=%async_computation.7 | async-start | bytes 2662400 | tf_op jit(solution)/shard_map/all_gather | solution.py:154
  17.8 32.9 %all-to-all-start = ((bf16[64,1,8,576]{3,2,1,0:T(8,128)(2,1)}), bf16[64,1,8,576]{3,2,1,0:T(8,128)(2,1)S(1)}, u32[]{:S(2)}, u32[]{:S(2)}) async-start(bf16[64,1,8,576]{3,2,1,0:T(8,128)(2,1)} %bitcast.57), calls=%async_computation | async-start | bytes 1310720 | tf_op jit(solution)/shard_map/all_to_all | solution.py:39
  29.4 157.3 %all-gather.5.cloned.1.call-start = ((), (), s32[]{:S(2)}) async-start(), calls=%async_computation.8 | async-start | bytes 2662400 | tf_op jit(solution)/shard_map/all_gather | solution.py:154
  30.4 75.2 %copy-start.6 = (s32[64]{0:T(128)S(1)}, s32[64]{0:T(128)}, u32[]{:S(2)}) copy-start(s32[64]{0:T(128)} %param.17) | copy-start | bytes 772
  53.4 52.2 %copy-start.2 = (bf16[8,8,576]{2,1,0:T(8,128)(2,1)}, bf16[8,8,576]{2,1,0:T(8,128)(2,1)S(1)}, u32[]{:S(2)}) copy-start(bf16[8,8,576]{2,1,0:T(8,128)(2,1)S(1)} %scatter_fusion.1) | copy-start | bytes 221188
  167.7 78.9 %all-to-all-start.1 = ((f32[1,1,64,2,16]{4,3,1,0,2:T(2,128)}), f32[1,1,64,2,16]{4,3,1,0,2:T(2,128)S(1)}, u32[]{:S(2)}, u32[]{:S(2)}) async-start(f32[1,1,64,2,16]{4,3,1,0,2:T(2,128)} %bitcast.61), calls=%async_computation.1 | async-start | bytes 131072 | tf_op jit(solution)/shard_map/all_to_all | solution.py:159
  391.1 7.4 %copy-start.5 = (bf16[2,1,2,576]{3,2,1,0:T(2,128)(2,1)S(1)}, bf16[2,1,2,576]{3,2,1,0:T(2,128)(2,1)}, u32[]{:S(2)}) copy-start(bf16[2,1,2,576]{3,2,1,0:T(2,128)(2,1)} %param.19) | copy-start | bytes 13828
  391.1 7.6 %copy-start.3 = (bf16[2,1,2,16,576]{4,3,2,1,0:T(8,128)(2,1)S(1)}, bf16[2,1,2,16,576]{4,3,2,1,0:T(8,128)(2,1)}, u32[]{:S(2)}) copy-start(bf16[2,1,2,16,576]{4,3,2,1,0:T(8,128)(2,1)} %param.18) | copy-start | bytes 221188
  391.1 102.1 %all-to-all-start.2 = ((f32[1,1,64,2,16,512]{5,4,3,1,0,2:T(8,128)}), f32[1,1,64,2,16,512]{5,4,3,1,0,2:T(8,128)}, u32[]{:S(2)}, u32[]{:S(2)}) async-start(f32[1,1,64,2,16,512]{5,4,3,1,0,2:T(8,128)} %bitcast.354), calls=%async_computation.2 | async-start | bytes 8388608 | tf_op jit(solution)/shard_map/all_to_all | solution.py:158
Sparse Core Ops, SparseCore 0:
  11.9 90.4 all-gather.2
  105.7 80.9 all-gather.4
where the time goes:
time: 505 us; the launch traced here: 503 us
  blocking collectives  171 us (34%)
  waiting for transfers between devices  140 us (28%)
  local copies, waits for them, and re-layouts  85.6 us (17%)
  matrix products  40.2 us (8%)
  starting transfers between devices  25.7 us (5%)
  other arithmetic  14.7 us (3%)
  between operations  14.3 us (3%)
  loops' own time  12.5 us (2%)
    all_to_all x1, blocking collectives, local(): lax.all_to_all(summed[None], 'pages', split_axis=2, concat_axis=0, tiled=...  100 us
    all_to_all x1, waiting for transfers between devices, local(): lax.all_to_all(summed[None], 'pages', split_axis=2, concat_axis=0, tiled=...  90.8 us
    all_gather x2, waiting for transfers between devices, local(): lax.all_gather(queries[step_index:step_index + 1], 'pages', axis=1, tiled...  35.3 us
    all_to_all x2, blocking collectives, local(): lax.all_to_all(weight_sum[None], 'pages', split_axis=2, concat_axis=0, ti...  27.5 us
    all_gather x1, blocking collectives, push_cache(): return (lax.all_gather(cache_part, 'heads', axis=1, tiled=True), cache_part)  26.2 us
    dot_general x16, matrix products, block_terms(): jnp.einsum('snrhc,nitc->snrhit', query_block, cached, preferred_element_t...  22.2 us
    gather x32, local copies, waits for them, and re-layouts, block_terms(): cached = cache_pool[page_table[page_ids, 1]]  21.2 us
    dot_general x16, matrix products, block_terms(): jnp.einsum('snrhit,nitc->snrhc', weights.astype(jnp.bfloat16), cached[......  17.5 us
  transfers between devices with their start and end apart: 5, of which 4 were waited for; matrix products, arithmetic and copies ran while one was open for 27% of the time, Pallas kernels for 0%

commit v1 on v0

v1 whole, which is shorter than its diff:
```python
import functools

import jax
import jax.numpy as jnp
from jax import lax
from jax.experimental import pallas as pl
from jax.experimental.pallas import tpu as pltpu
from jax.sharding import PartitionSpec as P

LAT = 512
LATW = 576
WIDE = 640
PAGE = 64
NY = 8
NQ = 8
NZ = 8
SHARE = 8
SOFTMAX_SCALE = 192.0 ** (-0.5)
MASKED_SCORE = -1e30
F32 = jnp.float32
BF16 = jnp.bfloat16
I32 = jnp.int32


def iota(shape, dim):
    return lax.broadcasted_iota(I32, shape, dim)


def dot(a, b):
    return jnp.dot(a, b, preferred_element_type=F32)


def dot_last(a, b):
    return lax.dot_general(a, b, (((1,), (1,)), ((), ())), preferred_element_type=F32)


def kernel(
    prefill, stretch, table, plist, lengths, queries, fresh,
    out, cache,
    pages, sorted_pages, row_pages, gathered, picked, keys, all_queries,
    sums, sums_in, stats, stats_in,
    load_sem, s1_send, s1_recv, right_send, right_recv, left_send, left_recv,
    s3_send, s3_recv, q_send, q_recv, s4_send, s4_recv, st_send, st_recv,
):
    p = lax.axis_index("pages")
    z = lax.axis_index("heads")
    y = p // NQ
    q = lax.rem(p, NQ)

    def in_row(i):
        return (y * NQ + i, z)

    def in_column(i):
        return (i * NQ + q, z)

    def in_depth(i):
        return (p, i)

    right, left = lax.rem(y + 1, NY), lax.rem(y + NY - 1, NY)
    row_peers = [lax.rem(q + o, NQ) for o in range(1, NQ)]
    depth_peers = [lax.rem(z + o, NZ) for o in range(1, NZ)]

    barrier = pltpu.get_barrier_semaphore()
    targets = [in_row(i) for i in row_peers] + [in_column(right), in_column(left)]
    targets += [in_depth(i) for i in depth_peers]
    for target in targets:
        pl.semaphore_signal(barrier, inc=1, device_id=target, device_id_type=pl.DeviceIdType.MESH)

    load = pltpu.make_async_copy(
        prefill.at[:, pl.ds(pl.multiple_of((z // 2) * 16, 16), 16), :], pages, load_sem
    )
    load.start()

    def remote(src, dst, send, recv, target):
        return pltpu.make_async_remote_copy(
            src_ref=src, dst_ref=dst, send_sem=send, recv_sem=recv,
            device_id=target, device_id_type=pl.DeviceIdType.MESH,
        )

    shift = table[0:1, 0:1]
    own_queries = queries[...].reshape(64, LATW)
    all_queries[z] = own_queries

    load.wait()
    lane = iota((1, 128), 1)
    page_of_lane = jnp.zeros((1, 128), I32)
    for k in range(8):
        page_of_lane = jnp.where(lane // 16 == k, stretch[p * 8 + k], page_of_lane)
    residue = (page_of_lane + shift) & 7
    row = iota((64, 128), 0)
    col = iota((64, 128), 1)
    chosen = jnp.logical_and(residue == row // 8, (col & 15) == (row & 7) + 8 * lax.rem(z, 2))
    page_col = jnp.sum(jnp.where(chosen, page_of_lane, 0).astype(F32), axis=1, keepdims=True)
    page_int = page_col.astype(I32)
    ordered = dot(chosen.astype(F32).astype(BF16), pages[...].reshape(128, LATW))
    sorted_pages[:, :, 0:LATW] = ordered.reshape(8, 8, LATW)
    tail = iota((64, 64), 1)
    marks = jnp.where(tail < 32, page_int // 8, page_int & 7).astype(F32)
    sorted_pages[:, :, LATW:WIDE] = marks.reshape(8, 8, WIDE - LATW)

    pl.semaphore_wait(barrier, len(targets))

    s1 = []
    for n, i in enumerate(row_peers):
        copy = remote(sorted_pages.at[i], row_pages.at[q], s1_send.at[n], s1_recv.at[n], in_row(i))
        copy.start()
        s1.append(copy)
    qc = []
    for n, i in enumerate(depth_peers):
        copy = remote(all_queries.at[z], all_queries.at[z], q_send.at[n], q_recv.at[n], in_depth(i))
        copy.start()
        qc.append(copy)
    row_pages[q] = sorted_pages[q]
    for copy in s1:
        copy.wait_recv()
    gathered[y] = row_pages[...].reshape(64, WIDE).astype(BF16)

    ring = []
    for step in range(4):
        if step:
            ring[-2].wait_recv()
            ring[-1].wait_recv()
        give_right = lax.rem(y + NY - step, NY)
        give_left = lax.rem(y + step, NY)
        rows_right = pl.ds(0, 64 if step < 3 else 32)
        rows_left = pl.ds(0, 64) if step < 3 else pl.ds(32, 32)
        view = gathered.at[give_right, rows_right, :]
        copy = remote(view, view, right_send.at[step], right_recv.at[step], in_column(right))
        copy.start()
        ring.append(copy)
        view = gathered.at[give_left, rows_left, :]
        copy = remote(view, view, left_send.at[step], left_recv.at[step], in_column(left))
        copy.start()
        ring.append(copy)
    ring[-2].wait_recv()
    ring[-1].wait_recv()

    have = gathered[...].reshape(512, WIDE)
    mark_lane = iota((64, WIDE), 1)
    weigh = jnp.where(mark_lane == LATW, 64.0, jnp.where(mark_lane == LATW + 32, 8.0, 0.0))
    have_key = dot_last(weigh.astype(BF16), have) + (iota((64, 512), 1) & 7).astype(F32)
    have_key = have_key.astype(I32)
    for half in range(2):
        first = jnp.zeros((256, 1), I32)
        dest = iota((256, 1), 0) // 64
        for i in range(4):
            first = jnp.where(dest == i, plist[y * NQ + half * 4 + i, 0], first)
        first = first + ((q - shift - first) & 7)
        inner = iota((256, 1), 0) & 63
        want = (first + 8 * (inner // 8)) * 8 + (inner & 7)
        key = jnp.concatenate([have_key] * 4, axis=0)
        pick = (want == key).astype(F32).astype(BF16)
        picked[pl.ds(half * 4, 4)] = dot(pick, have).astype(BF16).reshape(4, 64, WIDE)
    s3 = []
    for n, i in enumerate(row_peers):
        copy = remote(picked.at[i], keys.at[q], s3_send.at[n], s3_recv.at[n], in_row(i))
        copy.start()
        s3.append(copy)
    keys[q] = picked[q]

    page = iota((512, 64), 0)
    slot = iota((512, 64), 1) // 8
    here = jnp.logical_and(table[:, 0:1] == p, table[:, 1:2] == slot)
    number = jnp.where(iota((512, 128), 1) < 64, iota((512, 128), 0) // 8, iota((512, 128), 0) & 7)
    lookup = lax.dot_general(
        here.astype(F32).astype(BF16), number.astype(F32).astype(BF16),
        (((0,), (0,)), ((), ())), preferred_element_type=F32,
    )
    want = (lookup[:, 0:1] * 64.0 + lookup[:, 64:65] * 8.0).astype(I32) + (iota((64, 1), 0) & 7)
    pick = (want == have_key).astype(F32).astype(BF16)
    cache[...] = dot(pick, have)[:, 0:LATW].reshape(8, 8, LATW).astype(BF16)

    fresh_rows = jnp.zeros((16, LATW), F32)
    fresh_index = iota((16, LATW), 0)
    for m in range(4):
        one = fresh[m // 2, 0, m % 2 : m % 2 + 1, :].astype(F32)
        fresh_rows = jnp.where(fresh_index == m, one, fresh_rows)
    fresh_rows = fresh_rows.astype(BF16)
    fresh_scores = dot_last(own_queries, fresh_rows) * SOFTMAX_SCALE
    seen = iota((64, 16), 1) <= iota((64, 16), 0) // 16
    fresh_peak = jnp.max(jnp.where(seen, fresh_scores, MASKED_SCORE), axis=1, keepdims=True)
    fresh_weight = jnp.where(seen, jnp.exp(fresh_scores - fresh_peak), 0.0)
    fresh_total = jnp.sum(fresh_weight, axis=1, keepdims=True)
    fresh_sum = dot(fresh_weight.astype(BF16), fresh_rows[:, 0:LAT])

    begin = plist[p, 0]
    token = iota((1, 512), 1)
    position = ((token // 64 - shift - begin) & 7) + 8 * ((token & 63) // 8)
    live = position * PAGE + z * SHARE + (token & 7) < lengths[p]

    for copy in qc:
        copy.wait_recv()
    for copy in s3:
        copy.wait_recv()
    latents = keys[...].reshape(512, WIDE)
    narrow = latents[:, 0:LATW]
    values = latents[:, 0:LAT]

    s4 = []
    stat_lane = iota((64, 128), 1)
    for n in range(NZ):
        i = lax.rem(z + n + 1, NZ)
        scores = dot_last(all_queries[i], narrow) * SOFTMAX_SCALE
        scores = jnp.where(live, scores, MASKED_SCORE)
        peak = jnp.max(scores, axis=1, keepdims=True)
        weight = jnp.where(live, jnp.exp(scores - peak), 0.0)
        total = jnp.sum(weight, axis=1, keepdims=True)
        summed = dot(weight.astype(BF16), values)
        stat = jnp.where(stat_lane == 0, peak, jnp.where(stat_lane == 1, total, 0.0))
        stat = jnp.transpose(stat)[0:8, :]
        if n < NZ - 1:
            sums[i] = summed.astype(BF16)
            stats[i, :, 0:64] = stat
            stats[i, :, 64:128] = stat
            copy = remote(stats.at[i], stats_in.at[z], st_send.at[n], st_recv.at[n], in_depth(i))
            copy.start()
            s4.append(copy)
            copy = remote(sums.at[i], sums_in.at[z], s4_send.at[n], s4_recv.at[n], in_depth(i))
            copy.start()
            s4.append(copy)
        else:
            stats_in[z, :, 0:64] = stat
            stats_in[z, :, 64:128] = stat
            own_sum = summed
            own_peak = peak

    for copy in s4:
        copy.wait_recv()
    peaks = stats_in[:, 0, :]
    totals = stats_in[:, 1, :]
    shared_peak = jnp.max(peaks, axis=0, keepdims=True)
    spread = jnp.concatenate(
        [peaks, totals, jnp.broadcast_to(shared_peak, (8, 128)), jnp.zeros((104, 128), F32)], axis=0
    )
    spread = jnp.transpose(spread)[0:64, :]
    top = jnp.maximum(spread[:, 16:17], fresh_peak)
    fresh_scale = jnp.exp(fresh_peak - top)
    numerator = fresh_scale * fresh_sum + jnp.exp(own_peak - top) * own_sum
    denominator = fresh_scale * fresh_total
    for n in range(NZ):
        scale = jnp.exp(spread[:, n : n + 1] - top)
        denominator = denominator + scale * spread[:, 8 + n : 9 + n]
    sums_in[z] = jnp.zeros((64, LAT), BF16)
    for n in range(NZ):
        scale = jnp.exp(spread[:, n : n + 1] - top)
        numerator = numerator + scale * sums_in[n].astype(F32)
    out[...] = (numerator / denominator).astype(BF16).reshape(2, 1, 2, 16, LAT)

    for copy in s1 + qc + ring + s3 + s4:
        copy.wait_send()


def local(prefill_latent, stretch_page, page_table, page_list, lengths, queries, new_latent):
    vmem = pl.BlockSpec(memory_space=pltpu.VMEM)
    smem = pl.BlockSpec(memory_space=pltpu.SMEM)
    dma = pltpu.SemaphoreType.DMA
    return pl.pallas_call(
        kernel,
        out_shape=(
            jax.ShapeDtypeStruct((2, 1, 2, 16, LAT), BF16),
            jax.ShapeDtypeStruct((8, 8, LATW), BF16),
        ),
        in_specs=[pl.BlockSpec(memory_space=pl.ANY), smem, vmem, smem, smem, vmem, vmem],
        out_specs=(vmem, vmem),
        scratch_shapes=[
            pltpu.VMEM((8, 16, LATW), BF16),
            pltpu.VMEM((8, 8, WIDE), F32),
            pltpu.VMEM((8, 8, WIDE), F32),
            pltpu.VMEM((8, 64, WIDE), BF16),
            pltpu.VMEM((8, 64, WIDE), BF16),
            pltpu.VMEM((8, 64, WIDE), BF16),
            pltpu.VMEM((8, 64, LATW), BF16),
            pltpu.VMEM((8, 64, LAT), BF16),
            pltpu.VMEM((8, 64, LAT), BF16),
            pltpu.VMEM((8, 8, 128), F32),
            pltpu.VMEM((8, 8, 128), F32),
            dma, dma((7,)), dma((7,)), dma((4,)), dma((4,)), dma((4,)), dma((4,)),
            dma((7,)), dma((7,)), dma((7,)), dma((7,)), dma((7,)), dma((7,)), dma((7,)), dma((7,)),
        ],
        compiler_params=pltpu.CompilerParams(
            collective_id=0, has_side_effects=True, vmem_limit_bytes=40 * 1024 * 1024
        ),
        name="place_and_attend",
    )(prefill_latent, stretch_page, page_table, page_list, lengths, queries, new_latent)


def solution(mesh):
    in_specs = (
        P("pages", None, None),
        P(),
        P(),
        P(),
        P(),
        P(None, "pages", None, "heads", None),
        P(None, "pages", None, None),
    )
    out_specs = (P(None, "pages", None, "heads", None), P("pages", "heads", None))
    return jax.shard_map(local, mesh=mesh, in_specs=in_specs, out_specs=out_specs, check_vma=False)
```

time: 505 us -> 65.1 us (0.13)
  blocking collectives: 171 us -> 0 us
  waiting for transfers between devices: 140 us -> 0 us
  local copies, waits for them, and re-layouts: 85.6 us -> 3.25 us
  Pallas kernels: 0 us -> 60.9 us
  matrix products: 40.2 us -> 0 us
  starting transfers between devices: 25.7 us -> 0 us
  other arithmetic: 14.7 us -> 0 us
  between operations: 14.3 us -> 0.74 us
  loops' own time: 12.5 us -> 0 us
    all_to_all x4 -> x0, blocking collectives: 144 us -> none  [the longest x1 100 us: local(): lax.all_to_all(summed[None], 'pages', split_axis=2, concat_axis=0, tiled=...]
    all_to_all x3 -> x0, waiting for transfers between devices: 104 us -> none  [the longest x1 90.8 us: local(): lax.all_to_all(summed[None], 'pages', split_axis=2, concat_axis=0, tiled=...]
    pallas_call x0 -> x1, Pallas kernels: none -> 60.9 us  [local(): pl.pallas_call(kernel, out_shape=(jax.ShapeDtypeStruct((2, 1, 2, 16, LAT)...]
    gather x66 -> x0, local copies, waits for them, and re-layouts: 51.7 us -> none  [the longest x32 21.2 us: block_terms(): cached = cache_pool[page_table[page_ids, 1]]]
    dot_general x34 -> x0, matrix products: 40.2 us -> none  [the longest x16 22.2 us: block_terms(): jnp.einsum('snrhc,nitc->snrhit', query_block, cached, preferred_element_t...]
    all_gather x2 -> x0, waiting for transfers between devices: 35.3 us -> none  [local(): lax.all_gather(queries[step_index:step_index + 1], 'pages', axis=1, tiled...]
    all_gather x1 -> x0, blocking collectives: 26.2 us -> none  [push_cache(): return (lax.all_gather(cache_part, 'heads', axis=1, tiled=True), cache_part)]
    all_to_all x3 -> x0, starting transfers between devices: 25.6 us -> none  [the longest x1 11.6 us: push_cache(): lax.all_to_all(outgoing, 'pages', split_axis=0, concat_axis=0, tiled=True)]
  transfers between devices with their start and end apart: 5 -> 0, of which waited for: 4 -> 0; matrix products, arithmetic and copies ran while one was open for 27% -> 0% of each run, Pallas kernels for 0% -> 0%
where the time goes in v1:
time: 65.1 us; the launch traced here: 64.9 us
  Pallas kernels  60.9 us (94%)
  local copies, waits for them, and re-layouts  3.25 us (5%)
  between operations  0.74 us (1%)
    pallas_call x1, Pallas kernels, local(): pl.pallas_call(kernel, out_shape=(jax.ShapeDtypeStruct((2, 1, 2, 16, LAT)...  60.9 us
    unnamed x15, local copies, waits for them, and re-layouts  3.25 us

profile of v1, /device:TPU:1, one launch (start us, length us, event | category | flops | bytes accessed | tf_op | source)
XLA Modules:
  0.0 64.9 jit_solution(11414403215817482533)
XLA Ops:
  0.6 0.0 copy-start.3
  0.6 0.0 copy-start.1
  0.7 0.0 copy-start.5
  0.7 0.0 copy-start.2
  0.7 0.0 copy-start.4
  0.7 0.9 %copy.9.table = s32[512,2]{1,0:T(8,128)S(1)} copy(s32[512,2]{0,1:T(2,128)} %param.9) | data formatting | bytes 8192 | tf_op args[2]
  1.6 0.0 copy-done.3
  1.6 0.0 copy-done.1
  1.6 0.0 copy-done.5
  1.6 0.0 copy-done.2
  1.6 0.0 copy-done.4
  1.6 0.0 copy-start
  1.6 1.1 %copy-done = bf16[8,64,576]{2,1,0:T(8,128)(2,1)S(1)} copy-done((bf16[8,64,576]{2,1,0:T(8,128)(2,1)S(1)}, bf16[8,64,576]{2,1,0:T(8,128)(2,1)}, u32[]{:S(2)}) %copy-start) | copy-done | bytes 589848
  2.7 60.9 %place_and_attend.1 = (bf16[2,1,2,16,512]{4,3,2,1,0:T(8,128)(2,1)S(1)}, bf16[8,8,576]{2,1,0:T(8,128)(2,1)S(1)}) custom-call(bf16[8,64,576]{2,1,0:T(8,128)(2,1)S(1)} %copy-done, s32[512]{0:T(512)S(1)} %copy-done.4, s32[512,2]{1,0:T(8,128)S(1)} %copy.9.table, s32[64,64]{1,0:T(8,128)S(1)} %copy-done.2, s32[64]{0:T(128)S(1)} %copy-done.5, ...), custom_call_target="tpu_custom_call" | custom-call | tf_op jit(solution)/shard_map/place_and_attend/pallas_call | solution.py:257
  63.6 0.6 copy.12
  64.3 0.6 copy.13
Async XLA Ops:
  0.6 0.9 %copy-start.3 = (bf16[2,1,2,576]{3,2,1,0:T(2,128)(2,1)S(1)}, bf16[2,1,2,576]{3,2,1,0:T(2,128)(2,1)}, u32[]{:S(2)}) copy-start(bf16[2,1,2,576]{3,2,1,0:T(2,128)(2,1)} %fresh.1) | copy-start | bytes 13828
  0.6 0.9 %copy-start.1 = (bf16[2,1,2,16,576]{4,3,2,1,0:T(8,128)(2,1)S(1)}, bf16[2,1,2,16,576]{4,3,2,1,0:T(8,128)(2,1)}, u32[]{:S(2)}) copy-start(bf16[2,1,2,16,576]{4,3,2,1,0:T(8,128)(2,1)} %queries.1) | copy-start | bytes 221188
  0.7 0.9 %copy-start.5 = (s32[64]{0:T(128)S(1)}, s32[64]{0:T(128)}, u32[]{:S(2)}) copy-start(s32[64]{0:T(128)} %lengths.1) | copy-start | bytes 772
  0.7 0.9 %copy-start.2 = (s32[64,64]{1,0:T(8,128)S(1)}, s32[64,64]{1,0:T(8,128)}, u32[]{:S(2)}) copy-start(s32[64,64]{1,0:T(8,128)} %plist.1) | copy-start | bytes 49156
  0.7 0.9 %copy-start.4 = (s32[512]{0:T(512)S(1)}, s32[512]{0:T(512)}, u32[]{:S(2)}) copy-start(s32[512]{0:T(512)} %stretch.1) | copy-start | bytes 6148
  1.6 1.1 %copy-start = (bf16[8,64,576]{2,1,0:T(8,128)(2,1)S(1)}, bf16[8,64,576]{2,1,0:T(8,128)(2,1)}, u32[]{:S(2)}) copy-start(bf16[8,64,576]{2,1,0:T(8,128)(2,1)} %prefill.1) | copy-start | bytes 1769476

commit v2 on v1

v2 whole, which is shorter than its diff:
```python
import jax
import jax.numpy as jnp
from jax import lax
from jax.experimental import pallas as pl
from jax.experimental.pallas import tpu as pltpu
from jax.sharding import PartitionSpec as P

LAT = 512
LATW = 576
PAGE = 64
NY = 8
NQ = 8
NZ = 8
SHARE = 8
STARTS = (0, 256, 512)
WIDTHS = (256, 256, 128)
USED = (256, 256, 64)
SOFTMAX_SCALE = 192.0 ** (-0.5)
MASKED_SCORE = -1e30
F32 = jnp.float32
BF16 = jnp.bfloat16
I32 = jnp.int32
DEPTH_ORDER = (4, 3, 5, 2, 6, 1, 7)


def iota(shape, dim):
    return lax.broadcasted_iota(I32, shape, dim)


def dot(a, b):
    return jnp.dot(a, b, preferred_element_type=F32)


def dot_last(a, b):
    return lax.dot_general(a, b, (((1,), (1,)), ((), ())), preferred_element_type=F32)


def hot(mask):
    return mask.astype(F32).astype(BF16)


def kernel(
    prefill_hbm, stretch_hbm, stretch_row_hbm, table_hbm, plist_hbm, lengths_hbm, queries_hbm, fresh_hbm,
    out, cache,
    pages, stretch, stretch_row, table, plist, lengths, fresh,
    outgoing, incoming, all_queries, picks,
    gathered0, gathered1, gathered2, picked0, picked1, picked2, keys0, keys1, keys2,
    sums, sums_in, stats, stats_in,
    load_sem, s1_send, s1_recv, s2_send, s2_recv,
    s3_send, s3_recv, q_send, q_recv, s4_send, s4_recv, st_send, st_recv,
):
    gathered = (gathered0, gathered1, gathered2)
    picked = (picked0, picked1, picked2)
    keys = (keys0, keys1, keys2)
    p = lax.axis_index("pages")
    z = lax.axis_index("heads")
    y = p // NQ
    q = lax.rem(p, NQ)
    core = lax.rem(q, 2)

    def in_row(i):
        return (y * NQ + i, z)

    def in_column(step):
        return (lax.rem(y + NY + step, NY) * NQ + q, z)

    def in_depth(i):
        return (p, i)

    loads = []
    sources = (
        (prefill_hbm.at[:, pl.ds(pl.multiple_of((z // 2) * 16, 16), 16), :], pages),
        (stretch_hbm, stretch),
        (table_hbm, table),
        (queries_hbm.at[:, 0], all_queries.at[z]),
        (stretch_row_hbm, stretch_row),
        (plist_hbm.at[pl.ds(pl.multiple_of(y * NQ, NQ), NQ), :], plist),
        (lengths_hbm, lengths),
        (fresh_hbm, fresh),
    )
    for n, (src, dst) in enumerate(sources):
        copy = pltpu.make_async_copy(src, dst, load_sem.at[n])
        copy.start()
        loads.append(copy)

    barrier = pltpu.get_barrier_semaphore()
    row_peers = [lax.rem(q + o, NQ) for o in range(1, NQ)]
    depth_peers = [lax.rem(z + o, NZ) for o in DEPTH_ORDER]
    targets = [in_row(i) for i in row_peers] + [in_column(d) for d in (1, -1, 2, -2)]
    targets += [in_depth(i) for i in depth_peers]
    for target in targets:
        pl.semaphore_signal(barrier, inc=1, device_id=target, device_id_type=pl.DeviceIdType.MESH)

    def remote(src, dst, send, recv, target):
        return pltpu.make_async_remote_copy(
            src_ref=src, dst_ref=dst, send_sem=send, recv_sem=recv,
            device_id=target, device_id_type=pl.DeviceIdType.MESH,
        )

    for copy in loads[0:3]:
        copy.wait()
    shift = table[0:1, 0:1]
    lane = iota((1, 128), 1)
    page_of_lane = jnp.zeros((1, 128), I32)
    for k in range(8):
        page_of_lane = jnp.where(lane // 16 == k, stretch[p * 8 + k], page_of_lane)
    residue = (page_of_lane + shift) & 7
    row = iota((128, 128), 0)
    col = iota((128, 128), 1)
    chosen = jnp.logical_and(residue == row // 16, (col & 15) == (row & 7) + 8 * lax.rem(z, 2))
    ordered = dot(hot(chosen), pages[...].reshape(128, LATW)).astype(BF16).astype(F32)
    second = (iota((128, 256), 0) & 8) == 8
    body = jnp.where(second, ordered[:, 256:512], ordered[:, 0:256]).astype(BF16)
    outgoing[:, :, 0:256] = body.reshape(8, 16, 256)
    outgoing[:, :, 256:320] = ordered[:, 512:576].astype(BF16).reshape(8, 16, 64)
    outgoing[:, :, 320:384] = jnp.zeros((8, 16, 64), BF16)

    pl.semaphore_wait(barrier, len(targets))

    s1 = []
    for n, i in enumerate(row_peers):
        copy = remote(outgoing.at[i], incoming.at[q], s1_send.at[n], s1_recv.at[n], in_row(i))
        copy.start()
        s1.append(copy)
    incoming[q] = outgoing[q]

    for copy in loads[3:]:
        copy.wait()
    qc = []
    for n, i in enumerate(depth_peers):
        copy = remote(all_queries.at[z], all_queries.at[z], q_send.at[n], q_recv.at[n], in_depth(i))
        copy.start()
        qc.append(copy)
    numbers = stretch_row[...]
    mine = ((numbers + shift) & 7) == q
    parts = jnp.where(iota((8, 512), 0) == 0, numbers // 8, numbers & 7)
    parts = jnp.where(mine, parts, 0).astype(F32).astype(BF16)
    same = hot(iota((512, 512), 0) // 8 == iota((512, 512), 1) // 8)
    found = dot(parts, same)
    have_key = (found[0:1, :] * 64.0 + found[1:2, :] * 8.0).astype(I32) + (iota((1, 512), 1) & 7)
    for half in range(2):
        first = jnp.zeros((256, 1), I32)
        dest = iota((256, 1), 0) // 64
        for i in range(4):
            first = jnp.where(dest == i, plist[half * 4 + i, 0], first)
        first = first + ((q - shift - first) & 7)
        inner = iota((256, 1), 0) & 63
        want = (first + 8 * (inner // 8)) * 8 + (inner & 7)
        picks[pl.ds(half * 256, 256), :] = hot(want == have_key)

    for copy in s1:
        copy.wait_recv()
    arrived = incoming[...].astype(F32)
    gathered0[y] = arrived[:, 0:8, 0:256].reshape(64, 256).astype(BF16)
    gathered1[y] = arrived[:, 8:16, 0:256].reshape(64, 256).astype(BF16)
    gathered2[y] = arrived[:, 0:8, 256:384].reshape(64, 128).astype(BF16)

    s2 = []

    def along(c, kind, block, rows, step):
        view = gathered[c].at[lax.rem(block + NY, NY), pl.ds(rows[0], rows[1]), :]
        copy = remote(view, view, s2_send.at[c, kind], s2_recv.at[c, kind], in_column(step))
        copy.start()
        s2.append(copy)
        return copy

    near = []
    for c in range(3):
        near.append([
            along(c, 0, y, (0, 64), 2),
            along(c, 1, y, (0, 64), -2),
            along(c, 2, y, (0, 64), 1),
            along(c, 3, y, (0, 64), -1),
        ])
    far = []
    for c in range(3):
        near[c][0].wait_recv()
        below = [along(c, 4, y - 2, (0, 64), 1), along(c, 6, y - 2, (0, 32), 2)]
        near[c][1].wait_recv()
        far.append(below + [along(c, 5, y + 2, (0, 64), -1), along(c, 7, y + 2, (32, 32), -2)])

    own_queries = all_queries[z].reshape(64, LATW)
    fresh_rows = jnp.zeros((16, LATW), F32)
    fresh_index = iota((16, LATW), 0)
    for m in range(4):
        one = fresh[m // 2, 0, m % 2 : m % 2 + 1, :].astype(F32)
        fresh_rows = jnp.where(fresh_index == m, one, fresh_rows)
    fresh_rows = fresh_rows.astype(BF16)
    fresh_scores = dot_last(own_queries, fresh_rows) * SOFTMAX_SCALE
    seen = iota((64, 16), 1) <= iota((64, 16), 0) // 16
    fresh_peak = jnp.max(jnp.where(seen, fresh_scores, MASKED_SCORE), axis=1, keepdims=True)
    fresh_weight = jnp.where(seen, jnp.exp(fresh_scores - fresh_peak), 0.0)
    fresh_total = jnp.sum(fresh_weight, axis=1, keepdims=True)
    fresh_sum = dot(fresh_weight.astype(BF16), fresh_rows[:, 0:LAT])

    s3 = []

    def hand(c, m, parity):
        i = lax.rem(q // 2 + m, 4) * 2 + parity
        copy = remote(
            picked[c].at[i], keys[c].at[q], s3_send.at[c, m * 2 + parity], s3_recv.at[c, m * 2 + core], in_row(i)
        )
        copy.start()
        s3.append(copy)

    def hand_sibling(c):
        i = q + 1 - 2 * core
        copy = remote(picked[c].at[i], keys[c].at[q], s3_send.at[c, 0], s3_recv.at[c, 0], in_row(i))
        copy.start()
        s3.append(copy)

    def hand_core(c, parity):
        for m in (2, 1, 3):
            hand(c, m, parity)

    for c in range(3):
        for copy in near[c][2:] + far[c]:
            copy.wait_recv()
        have = gathered[c][...].reshape(512, WIDTHS[c])
        picked[c][...] = dot(picks[...], have).astype(BF16).reshape(8, 64, WIDTHS[c])
        if c < 2:
            hand_core(c, 0)
        if c == 0:
            hand_core(c, 1)
        hand_sibling(c)
        keys[c][q] = picked[c][q]
    hand_core(2, 0)
    hand_core(1, 1)
    hand_core(2, 1)

    slot = iota((64, 512), 0) // 8
    here = jnp.logical_and(table[0:1, :] == p, table[1:2, :] == slot)
    number = jnp.where(here, iota((64, 512), 1), 0).astype(F32)
    want = jnp.sum(number, axis=1, keepdims=True).astype(I32) * 8 + (iota((64, 1), 0) & 7)
    pick = hot(want == have_key)
    for c in range(3):
        have = gathered[c][...].reshape(512, WIDTHS[c])[:, 0 : USED[c]]
        rows = dot(pick, have).reshape(8, 8, USED[c]).astype(BF16)
        cache[:, :, STARTS[c] : STARTS[c] + USED[c]] = rows

    begin = plist[q, 0]
    token = iota((1, 512), 1)
    position = ((token // 64 - shift - begin) & 7) + 8 * ((token & 63) // 8)
    live = position * PAGE + z * SHARE + (token & 7) < lengths[p]

    for copy in qc:
        copy.wait_recv()
    for c in range(3):
        for n in range(8):
            if n == 1:
                continue
            if n == 0:
                source = q + 1 - 2 * core
            else:
                source = lax.rem(q // 2 + 4 - n // 2, 4) * 2 + n % 2
            remote(
                picked[c].at[source], keys[c].at[source], s3_send.at[c, n], s3_recv.at[c, n], in_row(source)
            ).wait_recv()
    latents = [keys[c][...].reshape(512, WIDTHS[c])[:, 0 : USED[c]] for c in range(3)]

    s4 = []
    s4_stats = []
    stat_lane = iota((64, 128), 1)
    for n in range(NZ):
        i = depth_peers[n] if n < NZ - 1 else z
        asked = all_queries[i].reshape(64, LATW)
        scores = dot_last(asked[:, 0:256], latents[0]) + dot_last(asked[:, 256:512], latents[1])
        scores = (scores + dot_last(asked[:, 512:576], latents[2])) * SOFTMAX_SCALE
        scores = jnp.where(live, scores, MASKED_SCORE)
        peak = jnp.max(scores, axis=1, keepdims=True)
        weight = jnp.where(live, jnp.exp(scores - peak), 0.0)
        total = jnp.sum(weight, axis=1, keepdims=True)
        weight = weight.astype(BF16)
        stat = jnp.where(stat_lane == 0, peak, jnp.where(stat_lane == 1, total, 0.0))
        stat = jnp.transpose(stat)[0:8, :]
        if n < NZ - 1:
            stats[i, :, 0:64] = stat
            stats[i, :, 64:128] = stat
            copy = remote(stats.at[i], stats_in.at[z], st_send.at[n], st_recv.at[n], in_depth(i))
            copy.start()
            s4_stats.append(copy)
            sums[i, :, 0:256] = dot(weight, latents[0]).astype(BF16)
            sums[i, :, 256:512] = dot(weight, latents[1]).astype(BF16)
            copy = remote(sums.at[i], sums_in.at[z], s4_send.at[n], s4_recv.at[n], in_depth(i))
            copy.start()
            s4.append(copy)
        else:
            stats_in[z, :, 0:64] = stat
            stats_in[z, :, 64:128] = stat
            own_sum = jnp.concatenate([dot(weight, latents[0]), dot(weight, latents[1])], axis=1)
            own_peak = peak

    for copy in s4_stats:
        copy.wait_recv()
    peaks = stats_in[:, 0, :]
    totals = stats_in[:, 1, :]
    shared_peak = jnp.max(peaks, axis=0, keepdims=True)
    scales = jnp.exp(peaks - shared_peak)
    shared_total = jnp.sum(scales * totals, axis=0, keepdims=True)
    spread = jnp.concatenate(
        [scales, jnp.broadcast_to(shared_peak, (8, 128)), jnp.broadcast_to(shared_total, (8, 128)),
         jnp.zeros((104, 128), F32)], axis=0
    )
    spread = jnp.transpose(spread)[0:64, :]
    cached_peak = spread[:, 8:9]
    top = jnp.maximum(cached_peak, fresh_peak)
    fresh_scale = jnp.exp(fresh_peak - top)
    cached_scale = jnp.exp(cached_peak - top)
    denominator = fresh_scale * fresh_total + cached_scale * spread[:, 16:17]
    numerator = fresh_scale * fresh_sum + jnp.exp(own_peak - top) * own_sum
    spread_lane = iota((64, 128), 1)
    for n, o in enumerate(DEPTH_ORDER):
        source = lax.rem(z + NZ - o, NZ)
        s4[n].wait_recv()
        scale = jnp.sum(jnp.where(spread_lane == source, spread, 0.0), axis=1, keepdims=True) * cached_scale
        numerator = numerator + scale * sums_in[source].astype(F32)
    out[...] = (numerator / denominator).astype(BF16).reshape(2, 1, 2, 16, LAT)

    for copy in s1 + qc + s2 + s3 + s4_stats + s4:
        copy.wait_send()


def local(prefill_latent, stretch_page, page_table, page_list, lengths, queries, new_latent):
    vmem = pl.BlockSpec(memory_space=pltpu.VMEM)
    hbm = pl.BlockSpec(memory_space=pltpu.HBM)
    dma = pltpu.SemaphoreType.DMA
    blocks = [pltpu.VMEM((8, 64, width), BF16) for width in WIDTHS]
    return pl.pallas_call(
        kernel,
        out_shape=(
            jax.ShapeDtypeStruct((2, 1, 2, 16, LAT), BF16),
            jax.ShapeDtypeStruct((8, 8, LATW), BF16),
        ),
        in_specs=[hbm] * 8,
        out_specs=(vmem, vmem),
        scratch_shapes=[
            pltpu.VMEM((8, 16, LATW), BF16),
            pltpu.SMEM((512,), I32),
            pltpu.VMEM((1, 512), I32),
            pltpu.VMEM((2, 512), I32),
            pltpu.SMEM((8, 64), I32),
            pltpu.SMEM((64,), I32),
            pltpu.VMEM((2, 1, 2, LATW), BF16),
            pltpu.VMEM((8, 16, 384), BF16),
            pltpu.VMEM((8, 16, 384), BF16),
            pltpu.VMEM((8, 2, 2, 16, LATW), BF16),
            pltpu.VMEM((512, 512), BF16),
            *blocks, *blocks, *blocks,
            pltpu.VMEM((8, 64, LAT), BF16),
            pltpu.VMEM((8, 64, LAT), BF16),
            pltpu.VMEM((8, 8, 128), F32),
            pltpu.VMEM((8, 8, 128), F32),
            dma((8,)), dma((7,)), dma((7,)), dma((3, 8)), dma((3, 8)),
            dma((3, 8)), dma((3, 8)), dma((7,)), dma((7,)), dma((7,)), dma((7,)), dma((7,)), dma((7,)),
        ],
        compiler_params=pltpu.CompilerParams(
            collective_id=0, has_side_effects=True, vmem_limit_bytes=24 * 1024 * 1024
        ),
        name="place_and_attend",
    )(*[pltpu.with_memory_space_constraint(x, pltpu.HBM) for x in (
        prefill_latent, stretch_page, stretch_page.reshape(1, 512), page_table.T, page_list, lengths,
        queries, new_latent)]
    )


def solution(mesh):
    in_specs = (
        P("pages", None, None),
        P(),
        P(),
        P(),
        P(),
        P(None, "pages", None, "heads", None),
        P(None, "pages", None, None),
    )
    out_specs = (P(None, "pages", None, "heads", None), P("pages", "heads", None))
    return jax.shard_map(local, mesh=mesh, in_specs=in_specs, out_specs=out_specs, check_vma=False)
```

time: 65.1 us -> 56.2 us (0.86)
  Pallas kernels: 60.9 us -> 54.1 us
  local copies, waits for them, and re-layouts: 3.25 us -> 1.27 us
    pallas_call x1, Pallas kernels: 60.9 us -> 54.1 us  [local(): pl.pallas_call(kernel, out_shape=(jax.ShapeDtypeStruct((2, 1, 2, 16, LAT)...]
    unnamed x15 -> x2, local copies, waits for them, and re-layouts: 3.25 us -> 1.27 us
where the time goes in v2:
time: 56.2 us; the launch traced here: 56 us
  Pallas kernels  54.1 us (96%)
  local copies, waits for them, and re-layouts  1.27 us (2%)
  between operations  0.64 us (1%)
    pallas_call x1, Pallas kernels, local(): pl.pallas_call(kernel, out_shape=(jax.ShapeDtypeStruct((2, 1, 2, 16, LAT)...  54.1 us
    unnamed x2, local copies, waits for them, and re-layouts  1.27 us

profile of v2, /device:TPU:1, one launch (start us, length us, event | category | flops | bytes accessed | tf_op | source)
XLA Modules:
  0.0 56.0 jit_solution(15796487539119079158)
XLA Ops:
  0.6 54.1 %place_and_attend.1 = (bf16[2,1,2,16,512]{4,3,2,1,0:T(8,128)(2,1)S(1)}, bf16[8,8,576]{2,1,0:T(8,128)(2,1)S(1)}) custom-call(bf16[8,64,576]{2,1,0:T(8,128)(2,1)} %prefill_hbm.1, s32[512]{0:T(512)} %stretch_hbm.1, s32[1,512]{1,0:T(1,128)} %bitcast.2, s32[2,512]{1,0:T(2,128)} %bitcast.3, s32[64,64]{1,0:T(8,128)} %plist_hbm.1, s32[64]{0:T(128)} %lengths_hbm.1, ...), custom_call_target="tpu_custom_call" | custom-call | tf_op jit(solution)/shard_map/place_and_attend/pallas_call | solution.py:328
  54.8 0.6 %copy.11 = bf16[2,1,2,16,512]{4,3,2,1,0:T(8,128)(2,1)} copy(bf16[2,1,2,16,512]{4,3,2,1,0:T(8,128)(2,1)S(1)} %get-tuple-element.4) | data formatting | bytes 131072
  55.4 0.6 %copy.12 = bf16[8,8,576]{2,1,0:T(8,128)(2,1)} copy(bf16[8,8,576]{2,1,0:T(8,128)(2,1)S(1)} %get-tuple-element.5) | data formatting | bytes 147456

commit v3 on v2

--- a/solution.py
+++ b/solution.py
@@ -12,15 +12,16 @@
 NQ = 8
 NZ = 8
 SHARE = 8
-STARTS = (0, 256, 512)
-WIDTHS = (256, 256, 128)
-USED = (256, 256, 64)
+STARTS = (512, 0, 256)
+WIDTHS = (128, 256, 256)
+USED = (64, 256, 256)
 SOFTMAX_SCALE = 192.0 ** (-0.5)
 MASKED_SCORE = -1e30
 F32 = jnp.float32
 BF16 = jnp.bfloat16
 I32 = jnp.int32
 DEPTH_ORDER = (4, 3, 5, 2, 6, 1, 7)
+BATCHES = ((3, 5, 4, 2), (6, 1, 7, 0))
 
 
 def iota(shape, dim):
@@ -47,7 +48,7 @@
     gathered0, gathered1, gathered2, picked0, picked1, picked2, keys0, keys1, keys2,
     sums, sums_in, stats, stats_in,
     load_sem, s1_send, s1_recv, s2_send, s2_recv,
-    s3_send, s3_recv, q_send, q_recv, s4_send, s4_recv, st_send, st_recv,
+    s3_send, s3_recv, q_send, q_recv, s4_send, s4_recv,
 ):
     gathered = (gathered0, gathered1, gathered2)
     picked = (picked0, picked1, picked2)
@@ -131,6 +132,42 @@
         copy = remote(all_queries.at[z], all_queries.at[z], q_send.at[n], q_recv.at[n], in_depth(i))
         copy.start()
         qc.append(copy)
+    for copy in s1:
+        copy.wait_recv()
+    arrived = incoming[...].astype(F32)
+    gathered0[y] = arrived[:, 0:8, 256:384].reshape(64, 128).astype(BF16)
+    gathered1[y] = arrived[:, 0:8, 0:256].reshape(64, 256).astype(BF16)
+    gathered2[y] = arrived[:, 8:16, 0:256].reshape(64, 256).astype(BF16)
+
+    s2 = []
+
+    def along(c, kind, block, rows, step):
+        view = gathered[c].at[lax.rem(block + NY, NY), pl.ds(rows[0], rows[1]), :]
+        copy = remote(view, view, s2_send.at[c, kind], s2_recv.at[c, kind], in_column(step))
+        copy.start()
+        s2.append(copy)
+        return copy
+
+    near = []
+    far = []
+
+    def start_near(c):
+        near.append([
+            along(c, 0, y, (0, 64), 2),
+            along(c, 1, y, (0, 64), -2),
+            along(c, 2, y, (0, 64), 1),
+            along(c, 3, y, (0, 64), -1),
+        ])
+
+    def start_far(c):
+        near[c][0].wait_recv()
+        below = [along(c, 4, y - 2, (0, 64), 1), along(c, 6, y - 2, (0, 32), 2)]
+        near[c][1].wait_recv()
+        far.append(below + [along(c, 5, y + 2, (0, 64), -1), along(c, 7, y + 2, (32, 32), -2)])
+
+    start_near(0)
+    start_near(1)
+
     numbers = stretch_row[...]
     mine = ((numbers + shift) & 7) == q
     parts = jnp.where(iota((8, 512), 0) == 0, numbers // 8, numbers & 7)
@@ -148,36 +185,10 @@
         want = (first + 8 * (inner // 8)) * 8 + (inner & 7)
         picks[pl.ds(half * 256, 256), :] = hot(want == have_key)
 
-    for copy in s1:
-        copy.wait_recv()
-    arrived = incoming[...].astype(F32)
-    gathered0[y] = arrived[:, 0:8, 0:256].reshape(64, 256).astype(BF16)
-    gathered1[y] = arrived[:, 8:16, 0:256].reshape(64, 256).astype(BF16)
-    gathered2[y] = arrived[:, 0:8, 256:384].reshape(64, 128).astype(BF16)
-
-    s2 = []
-
-    def along(c, kind, block, rows, step):
-        view = gathered[c].at[lax.rem(block + NY, NY), pl.ds(rows[0], rows[1]), :]
-        copy = remote(view, view, s2_send.at[c, kind], s2_recv.at[c, kind], in_column(step))
-        copy.start()
-        s2.append(copy)
-        return copy
-
-    near = []
-    for c in range(3):
-        near.append([
-            along(c, 0, y, (0, 64), 2),
-            along(c, 1, y, (0, 64), -2),
-            along(c, 2, y, (0, 64), 1),
-            along(c, 3, y, (0, 64), -1),
-        ])
-    far = []
-    for c in range(3):
-        near[c][0].wait_recv()
-        below = [along(c, 4, y - 2, (0, 64), 1), along(c, 6, y - 2, (0, 32), 2)]
-        near[c][1].wait_recv()
-        far.append(below + [along(c, 5, y + 2, (0, 64), -1), along(c, 7, y + 2, (32, 32), -2)])
+    start_far(0)
+    start_near(2)
+    start_far(1)
+    start_far(2)
 
     own_queries = all_queries[z].reshape(64, LATW)
     fresh_rows = jnp.zeros((16, LATW), F32)
@@ -218,15 +229,10 @@
             copy.wait_recv()
         have = gathered[c][...].reshape(512, WIDTHS[c])
         picked[c][...] = dot(picks[...], have).astype(BF16).reshape(8, 64, WIDTHS[c])
-        if c < 2:
-            hand_core(c, 0)
-        if c == 0:
-            hand_core(c, 1)
+        hand_core(c, 0)
+        hand_core(c, 1)
         hand_sibling(c)
         keys[c][q] = picked[c][q]
-    hand_core(2, 0)
-    hand_core(1, 1)
-    hand_core(2, 1)
 
     slot = iota((64, 512), 0) // 8
     here = jnp.logical_and(table[0:1, :] == p, table[1:2, :] == slot)
@@ -259,64 +265,120 @@
     latents = [keys[c][...].reshape(512, WIDTHS[c])[:, 0 : USED[c]] for c in range(3)]
 
     s4 = []
-    s4_stats = []
-    stat_lane = iota((64, 128), 1)
-    for n in range(NZ):
-        i = depth_peers[n] if n < NZ - 1 else z
-        asked = all_queries[i].reshape(64, LATW)
-        scores = dot_last(asked[:, 0:256], latents[0]) + dot_last(asked[:, 256:512], latents[1])
-        scores = (scores + dot_last(asked[:, 512:576], latents[2])) * SOFTMAX_SCALE
+
+    def send(n, src, dst, target):
+        copy = remote(src, dst, s4_send.at[n], s4_recv.at[n], in_depth(target))
+        copy.start()
+        s4.append(copy)
+        return copy
+
+    def stat_block(peak, total):
+        lane = iota((64, 128), 1)
+        block = jnp.transpose(jnp.where(lane == 0, peak, jnp.where(lane == 1, total, 0.0)))[0:8, :]
+        return jnp.concatenate([block, block], axis=1)
+
+    def share(offsets):
+        asked = jnp.concatenate([all_queries[depth[o]].reshape(64, LATW) for o in offsets], axis=0)
+        scores = dot_last(asked[:, 0:256], latents[1]) + dot_last(asked[:, 256:512], latents[2])
+        scores = (scores + dot_last(asked[:, 512:576], latents[0])) * SOFTMAX_SCALE
         scores = jnp.where(live, scores, MASKED_SCORE)
         peak = jnp.max(scores, axis=1, keepdims=True)
         weight = jnp.where(live, jnp.exp(scores - peak), 0.0)
         total = jnp.sum(weight, axis=1, keepdims=True)
         weight = weight.astype(BF16)
-        stat = jnp.where(stat_lane == 0, peak, jnp.where(stat_lane == 1, total, 0.0))
-        stat = jnp.transpose(stat)[0:8, :]
-        if n < NZ - 1:
-            stats[i, :, 0:64] = stat
-            stats[i, :, 64:128] = stat
-            copy = remote(stats.at[i], stats_in.at[z], st_send.at[n], st_recv.at[n], in_depth(i))
-            copy.start()
-            s4_stats.append(copy)
-            sums[i, :, 0:256] = dot(weight, latents[0]).astype(BF16)
-            sums[i, :, 256:512] = dot(weight, latents[1]).astype(BF16)
-            copy = remote(sums.at[i], sums_in.at[z], s4_send.at[n], s4_recv.at[n], in_depth(i))
-            copy.start()
-            s4.append(copy)
-        else:
-            stats_in[z, :, 0:64] = stat
-            stats_in[z, :, 64:128] = stat
-            own_sum = jnp.concatenate([dot(weight, latents[0]), dot(weight, latents[1])], axis=1)
-            own_peak = peak
-
-    for copy in s4_stats:
-        copy.wait_recv()
-    peaks = stats_in[:, 0, :]
-    totals = stats_in[:, 1, :]
-    shared_peak = jnp.max(peaks, axis=0, keepdims=True)
-    scales = jnp.exp(peaks - shared_peak)
-    shared_total = jnp.sum(scales * totals, axis=0, keepdims=True)
-    spread = jnp.concatenate(
-        [scales, jnp.broadcast_to(shared_peak, (8, 128)), jnp.broadcast_to(shared_total, (8, 128)),
-         jnp.zeros((104, 128), F32)], axis=0
-    )
-    spread = jnp.transpose(spread)[0:64, :]
-    cached_peak = spread[:, 8:9]
-    top = jnp.maximum(cached_peak, fresh_peak)
+        summed = [dot(weight, latents[1]), dot(weight, latents[2])]
+        terms = {}
+        for k, o in enumerate(offsets):
+            rows = slice(64 * k, 64 * k + 64)
+            terms[o] = (jnp.concatenate([part[rows] for part in summed], axis=1), peak[rows], total[rows])
+        return terms
+
+    depth = [lax.rem(z + o, NZ) for o in range(NZ)]
+    arrivals = {}
+    terms = share(BATCHES[0])
+    for o in (3, 5, 4):
+        summed, peak, total = terms[o]
+        sums[o] = summed.astype(BF16)
+        stats[o] = stat_block(peak, total)
+    arrivals["stat3"] = send(0, stats.at[3], stats_in.at[0], depth[1])
+    arrivals["stat5"] = send(1, stats.at[5], stats_in.at[1], depth[7])
+    arrivals["stat4"] = send(2, stats.at[4], stats_in.at[2], depth[2])
+    arrivals["stat4b"] = send(3, stats.at[4], stats_in.at[3], depth[6])
+    arrivals["sum3"] = send(4, sums.at[3], sums_in.at[0], depth[1])
+    arrivals["sum5"] = send(5, sums.at[5], sums_in.at[1], depth[7])
+    arrivals["sum4"] = send(6, sums.at[4, pl.ds(0, 32), :], sums_in.at[2, pl.ds(0, 32), :], depth[2])
+    arrivals["sum4b"] = send(7, sums.at[4, pl.ds(32, 32), :], sums_in.at[2, pl.ds(32, 32), :], depth[6])
+    ahead = terms[2]
+    terms = share(BATCHES[1])
+    behind = terms[6]
+    for o in (1, 7):
+        summed, peak, total = terms[o]
+        sums[o] = summed.astype(BF16)
+        stats[o] = stat_block(peak, total)
+    arrivals["stat1"] = send(8, stats.at[1], stats_in.at[4], depth[1])
+    arrivals["stat7"] = send(9, stats.at[7], stats_in.at[5], depth[7])
+    arrivals["sum1"] = send(10, sums.at[1], sums_in.at[3], depth[1])
+    arrivals["sum7"] = send(11, sums.at[7], sums_in.at[4], depth[7])
+    own_sum, own_peak, own_total = terms[0]
+
+    def columns(blocks):
+        filled = jnp.concatenate(blocks + [jnp.zeros((128 - 8 * len(blocks), 128), F32)], axis=0)
+        return jnp.transpose(filled)[0:64, :]
+
+    def relay(own, full, half, first_rows):
+        own_sum, own_peak, own_total = own
+        arrivals["stat3" if first_rows else "stat5"].wait_recv()
+        arrivals["stat4" if first_rows else "stat4b"].wait_recv()
+        spread = columns([stats_in[full], stats_in[half]])
+        inside = iota((64, 1), 0) < 32
+        if not first_rows:
+            inside = jnp.logical_not(inside)
+        full_peak = spread[:, 0:1]
+        half_peak = jnp.where(inside, spread[:, 8:9], MASKED_SCORE)
+        half_total = jnp.where(inside, spread[:, 9:10], 0.0)
+        peak = jnp.maximum(jnp.maximum(own_peak, full_peak), half_peak)
+        own_scale = jnp.exp(own_peak - peak)
+        full_scale = jnp.exp(full_peak - peak)
+        half_scale = jnp.exp(half_peak - peak)
+        total = own_scale * own_total + full_scale * spread[:, 1:2] + half_scale * half_total
+        arrivals["sum3" if first_rows else "sum5"].wait_recv()
+        merged = own_scale * own_sum + full_scale * sums_in[full].astype(F32)
+        arrivals["sum4" if first_rows else "sum4b"].wait_recv()
+        rows = slice(0, 32) if first_rows else slice(32, 64)
+        extra = half_scale[rows] * sums_in[2, rows, :].astype(F32)
+        pieces = [merged[0:32], merged[32:64]]
+        pieces[0 if first_rows else 1] = pieces[0 if first_rows else 1] + extra
+        return jnp.concatenate(pieces, axis=0), peak, total
+
+    for n, (own, full, half, first_rows) in enumerate(((ahead, 0, 2, True), (behind, 1, 3, False))):
+        summed, peak, total = relay(own, full, half, first_rows)
+        o = 2 if first_rows else 6
+        stats[o] = stat_block(peak, total)
+        arrivals["stat%d" % o] = send(12 + n, stats.at[o], stats_in.at[6 + n], depth[o])
+        sums[o] = summed.astype(BF16)
+        arrivals["sum%d" % o] = send(14 + n, sums.at[o], sums_in.at[5 + n], depth[o])
+
+    for name in ("stat1", "stat7", "stat2", "stat6"):
+        arrivals[name].wait_recv()
+    spread = columns([stats_in[k] for k in (4, 5, 6, 7)])
+    peaks = [spread[:, 8 * k : 8 * k + 1] for k in range(4)]
+    totals = [spread[:, 8 * k + 1 : 8 * k + 2] for k in range(4)]
+    top = jnp.maximum(own_peak, fresh_peak)
+    for peak in peaks:
+        top = jnp.maximum(top, peak)
     fresh_scale = jnp.exp(fresh_peak - top)
-    cached_scale = jnp.exp(cached_peak - top)
-    denominator = fresh_scale * fresh_total + cached_scale * spread[:, 16:17]
-    numerator = fresh_scale * fresh_sum + jnp.exp(own_peak - top) * own_sum
-    spread_lane = iota((64, 128), 1)
-    for n, o in enumerate(DEPTH_ORDER):
-        source = lax.rem(z + NZ - o, NZ)
-        s4[n].wait_recv()
-        scale = jnp.sum(jnp.where(spread_lane == source, spread, 0.0), axis=1, keepdims=True) * cached_scale
-        numerator = numerator + scale * sums_in[source].astype(F32)
+    own_scale = jnp.exp(own_peak - top)
+    scales = [jnp.exp(peak - top) for peak in peaks]
+    denominator = fresh_scale * fresh_total + own_scale * own_total
+    for scale, total in zip(scales, totals):
+        denominator = denominator + scale * total
+    numerator = fresh_scale * fresh_sum + own_scale * own_sum
+    for k, name in enumerate(("sum1", "sum7", "sum2", "sum6")):
+        arrivals[name].wait_recv()
+        numerator = numerator + scales[k] * sums_in[3 + k].astype(F32)
     out[...] = (numerator / denominator).astype(BF16).reshape(2, 1, 2, 16, LAT)
 
-    for copy in s1 + qc + s2 + s3 + s4_stats + s4:
+    for copy in s1 + qc + s2 + s3 + s4:
         copy.wait_send()
 
 
@@ -351,7 +413,7 @@
             pltpu.VMEM((8, 8, 128), F32),
             pltpu.VMEM((8, 8, 128), F32),
             dma((8,)), dma((7,)), dma((7,)), dma((3, 8)), dma((3, 8)),
-            dma((3, 8)), dma((3, 8)), dma((7,)), dma((7,)), dma((7,)), dma((7,)), dma((7,)), dma((7,)),
+            dma((3, 8)), dma((3, 8)), dma((7,)), dma((7,)), dma((16,)), dma((16,)),
         ],
         compiler_params=pltpu.CompilerParams(
             collective_id=0, has_side_effects=True, vmem_limit_bytes=24 * 1024 * 1024

time: 56.2 us -> 51 us (0.907)
  the two profiles are of different devices: /device:TPU:1 before, /device:TPU:2 now
where the time goes in v3:
time: 51 us; the launch traced here: 50.9 us
  Pallas kernels  49 us (96%)
  local copies, waits for them, and re-layouts  1.27 us (2%)
  between operations  0.64 us (1%)
    pallas_call x1, Pallas kernels, local(): pl.pallas_call(kernel, out_shape=(jax.ShapeDtypeStruct((2, 1, 2, 16, LAT)...  49 us
    unnamed x2, local copies, waits for them, and re-layouts  1.27 us

profile of v3, /device:TPU:2, one launch (start us, length us, event | category | flops | bytes accessed | tf_op | source)
XLA Modules:
  0.0 50.9 jit_solution(7865410228324236525)
XLA Ops:
  0.6 49.0 %place_and_attend.1 = (bf16[2,1,2,16,512]{4,3,2,1,0:T(8,128)(2,1)S(1)}, bf16[8,8,576]{2,1,0:T(8,128)(2,1)S(1)}) custom-call(bf16[8,64,576]{2,1,0:T(8,128)(2,1)} %prefill_hbm.1, s32[512]{0:T(512)} %stretch_hbm.1, s32[1,512]{1,0:T(1,128)} %bitcast.2, s32[2,512]{1,0:T(2,128)} %bitcast.3, s32[64,64]{1,0:T(8,128)} %plist_hbm.1, s32[64]{0:T(128)} %lengths_hbm.1, ...), custom_call_target="tpu_custom_call" | custom-call | tf_op jit(solution)/shard_map/place_and_attend/pallas_call | solution.py:390
  49.6 0.6 %copy.11 = bf16[2,1,2,16,512]{4,3,2,1,0:T(8,128)(2,1)} copy(bf16[2,1,2,16,512]{4,3,2,1,0:T(8,128)(2,1)S(1)} %get-tuple-element.4) | data formatting | bytes 131072
  50.3 0.6 %copy.12 = bf16[8,8,576]{2,1,0:T(8,128)(2,1)} copy(bf16[8,8,576]{2,1,0:T(8,128)(2,1)S(1)} %get-tuple-element.5) | data formatting | bytes 147456

commit v4 on v3

--- a/solution.py
+++ b/solution.py
@@ -12,14 +12,26 @@
 NQ = 8
 NZ = 8
 SHARE = 8
-STARTS = (512, 0, 256)
-WIDTHS = (128, 256, 256)
-USED = (64, 256, 256)
+WIDE = 640
+CHUNKS = ((512, 128), (0, 256), (256, 256))
 SOFTMAX_SCALE = 192.0 ** (-0.5)
 MASKED_SCORE = -1e30
 F32 = jnp.float32
 BF16 = jnp.bfloat16
 I32 = jnp.int32
+FIRST = 2
+ORDER = (
+    ("near", 0),
+    ("near", 1),
+    ("far", 0),
+    ("near", 2),
+    ("far", 1),
+    ("pass", 0),
+    ("far", 2),
+    ("pass", 1),
+    ("pass", 2),
+)
+HALVES = (pl.ds(0, 256), pl.ds(256, 256))
 DEPTH_ORDER = (4, 3, 5, 2, 6, 1, 7)
 BATCHES = ((3, 5, 4, 2), (6, 1, 7, 0))
 
@@ -45,14 +57,12 @@
     out, cache,
     pages, stretch, stretch_row, table, plist, lengths, fresh,
     outgoing, incoming, all_queries, picks,
-    gathered0, gathered1, gathered2, picked0, picked1, picked2, keys0, keys1, keys2,
     sums, sums_in, stats, stats_in,
     load_sem, s1_send, s1_recv, s2_send, s2_recv,
-    s3_send, s3_recv, q_send, q_recv, s4_send, s4_recv,
+    s3_send, s3_recv, q_send, q_recv, s4_send, s4_recv, *blocks,
 ):
-    gathered = (gathered0, gathered1, gathered2)
-    picked = (picked0, picked1, picked2)
-    keys = (keys0, keys1, keys2)
+    chunks = len(CHUNKS)
+    gathered, picked, keys = blocks[:chunks], blocks[chunks : 2 * chunks], blocks[2 * chunks :]
     p = lax.axis_index("pages")
     z = lax.axis_index("heads")
     y = p // NQ
@@ -135,9 +145,10 @@
     for copy in s1:
         copy.wait_recv()
     arrived = incoming[...].astype(F32)
-    gathered0[y] = arrived[:, 0:8, 256:384].reshape(64, 128).astype(BF16)
-    gathered1[y] = arrived[:, 0:8, 0:256].reshape(64, 256).astype(BF16)
-    gathered2[y] = arrived[:, 8:16, 0:256].reshape(64, 256).astype(BF16)
+    whole = jnp.concatenate([arrived[:, 0:8, 0:256], arrived[:, 8:16, 0:256], arrived[:, 0:8, 256:384]], axis=2)
+    whole = whole.reshape(64, WIDE).astype(BF16)
+    for c, (start, width) in enumerate(CHUNKS):
+        gathered[c][y] = whole[:, start : start + width]
 
     s2 = []
 
@@ -165,8 +176,43 @@
         near[c][1].wait_recv()
         far.append(below + [along(c, 5, y + 2, (0, 64), -1), along(c, 7, y + 2, (32, 32), -2)])
 
-    start_near(0)
-    start_near(1)
+    s3 = []
+
+    def part(ref, i, c):
+        return ref[c].at[i]
+
+    def hand(c, m, parity):
+        i = lax.rem(q // 2 + m, 4) * 2 + parity
+        copy = remote(
+            part(picked, i, c), part(keys, q, c), s3_send.at[c, m * 2 + parity], s3_recv.at[c, m * 2 + core], in_row(i)
+        )
+        copy.start()
+        s3.append(copy)
+
+    def hand_sibling(c):
+        i = q + 1 - 2 * core
+        copy = remote(part(picked, i, c), part(keys, q, c), s3_send.at[c, 0], s3_recv.at[c, 0], in_row(i))
+        copy.start()
+        s3.append(copy)
+
+    def hand_core(c, parity):
+        for m in (2, 1, 3):
+            hand(c, m, parity)
+
+    def pass_on(c):
+        for copy in near[c][2:] + far[c]:
+            copy.wait_recv()
+        width = CHUNKS[c][1]
+        have = gathered[c][...].reshape(512, width)
+        picked[c][...] = dot(picks[...], have).astype(BF16).reshape(8, 64, width)
+        hand_core(c, 0)
+        hand_core(c, 1)
+        hand_sibling(c)
+        keys[c][q] = picked[c][q]
+
+    start = {"near": start_near, "far": start_far, "pass": pass_on}
+    for kind, c in ORDER[:FIRST]:
+        start[kind](c)
 
     numbers = stretch_row[...]
     mine = ((numbers + shift) & 7) == q
@@ -185,10 +231,8 @@
         want = (first + 8 * (inner // 8)) * 8 + (inner & 7)
         picks[pl.ds(half * 256, 256), :] = hot(want == have_key)
 
-    start_far(0)
-    start_near(2)
-    start_far(1)
-    start_far(2)
+    for kind, c in ORDER[FIRST:]:
+        start[kind](c)
 
     own_queries = all_queries[z].reshape(64, LATW)
     fresh_rows = jnp.zeros((16, LATW), F32)
@@ -204,45 +248,16 @@
     fresh_total = jnp.sum(fresh_weight, axis=1, keepdims=True)
     fresh_sum = dot(fresh_weight.astype(BF16), fresh_rows[:, 0:LAT])
 
-    s3 = []
-
-    def hand(c, m, parity):
-        i = lax.rem(q // 2 + m, 4) * 2 + parity
-        copy = remote(
-            picked[c].at[i], keys[c].at[q], s3_send.at[c, m * 2 + parity], s3_recv.at[c, m * 2 + core], in_row(i)
-        )
-        copy.start()
-        s3.append(copy)
-
-    def hand_sibling(c):
-        i = q + 1 - 2 * core
-        copy = remote(picked[c].at[i], keys[c].at[q], s3_send.at[c, 0], s3_recv.at[c, 0], in_row(i))
-        copy.start()
-        s3.append(copy)
-
-    def hand_core(c, parity):
-        for m in (2, 1, 3):
-            hand(c, m, parity)
-
-    for c in range(3):
-        for copy in near[c][2:] + far[c]:
-            copy.wait_recv()
-        have = gathered[c][...].reshape(512, WIDTHS[c])
-        picked[c][...] = dot(picks[...], have).astype(BF16).reshape(8, 64, WIDTHS[c])
-        hand_core(c, 0)
-        hand_core(c, 1)
-        hand_sibling(c)
-        keys[c][q] = picked[c][q]
+    def joined(refs):
+        order = sorted(range(chunks), key=lambda c: CHUNKS[c][0])
+        return jnp.concatenate([refs[c][...].reshape(512, CHUNKS[c][1]) for c in order], axis=1)
 
     slot = iota((64, 512), 0) // 8
     here = jnp.logical_and(table[0:1, :] == p, table[1:2, :] == slot)
     number = jnp.where(here, iota((64, 512), 1), 0).astype(F32)
     want = jnp.sum(number, axis=1, keepdims=True).astype(I32) * 8 + (iota((64, 1), 0) & 7)
     pick = hot(want == have_key)
-    for c in range(3):
-        have = gathered[c][...].reshape(512, WIDTHS[c])[:, 0 : USED[c]]
-        rows = dot(pick, have).reshape(8, 8, USED[c]).astype(BF16)
-        cache[:, :, STARTS[c] : STARTS[c] + USED[c]] = rows
+    cache[...] = dot(pick, joined(gathered)[:, 0:LATW]).reshape(8, 8, LATW).astype(BF16)
 
     begin = plist[q, 0]
     token = iota((1, 512), 1)
@@ -251,7 +266,7 @@
 
     for copy in qc:
         copy.wait_recv()
-    for c in range(3):
+    for c in range(len(CHUNKS)):
         for n in range(8):
             if n == 1:
                 continue
@@ -260,9 +275,11 @@
             else:
                 source = lax.rem(q // 2 + 4 - n // 2, 4) * 2 + n % 2
             remote(
-                picked[c].at[source], keys[c].at[source], s3_send.at[c, n], s3_recv.at[c, n], in_row(source)
+                part(picked, source, c), part(keys, source, c), s3_send.at[c, n], s3_recv.at[c, n], in_row(source)
             ).wait_recv()
-    latents = [keys[c][...].reshape(512, WIDTHS[c])[:, 0 : USED[c]] for c in range(3)]
+    latents = joined(keys)
+    narrow = latents[:, 0:LATW]
+    values = latents[:, 0:LAT]
 
     s4 = []
 
@@ -279,18 +296,17 @@
 
     def share(offsets):
         asked = jnp.concatenate([all_queries[depth[o]].reshape(64, LATW) for o in offsets], axis=0)
-        scores = dot_last(asked[:, 0:256], latents[1]) + dot_last(asked[:, 256:512], latents[2])
-        scores = (scores + dot_last(asked[:, 512:576], latents[0])) * SOFTMAX_SCALE
+        scores = dot_last(asked, narrow) * SOFTMAX_SCALE
         scores = jnp.where(live, scores, MASKED_SCORE)
         peak = jnp.max(scores, axis=1, keepdims=True)
         weight = jnp.where(live, jnp.exp(scores - peak), 0.0)
         total = jnp.sum(weight, axis=1, keepdims=True)
         weight = weight.astype(BF16)
-        summed = [dot(weight, latents[1]), dot(weight, latents[2])]
+        summed = dot(weight, values)
         terms = {}
         for k, o in enumerate(offsets):
             rows = slice(64 * k, 64 * k + 64)
-            terms[o] = (jnp.concatenate([part[rows] for part in summed], axis=1), peak[rows], total[rows])
+            terms[o] = (summed[rows], peak[rows], total[rows])
         return terms
 
     depth = [lax.rem(z + o, NZ) for o in range(NZ)]
@@ -304,10 +320,12 @@
     arrivals["stat5"] = send(1, stats.at[5], stats_in.at[1], depth[7])
     arrivals["stat4"] = send(2, stats.at[4], stats_in.at[2], depth[2])
     arrivals["stat4b"] = send(3, stats.at[4], stats_in.at[3], depth[6])
-    arrivals["sum3"] = send(4, sums.at[3], sums_in.at[0], depth[1])
-    arrivals["sum5"] = send(5, sums.at[5], sums_in.at[1], depth[7])
-    arrivals["sum4"] = send(6, sums.at[4, pl.ds(0, 32), :], sums_in.at[2, pl.ds(0, 32), :], depth[2])
-    arrivals["sum4b"] = send(7, sums.at[4, pl.ds(32, 32), :], sums_in.at[2, pl.ds(32, 32), :], depth[6])
+    for h, lanes in enumerate(HALVES):
+        arrivals["sum3", h] = send(8 + h, sums.at[3, :, lanes], sums_in.at[0, :, lanes], depth[1])
+        arrivals["sum5", h] = send(12 + h, sums.at[5, :, lanes], sums_in.at[1, :, lanes], depth[7])
+        top_rows, low_rows = pl.ds(0, 32), pl.ds(32, 32)
+        arrivals["sum4", h] = send(16 + h, sums.at[4, top_rows, lanes], sums_in.at[2, top_rows, lanes], depth[2])
+        arrivals["sum4b", h] = send(20 + h, sums.at[4, low_rows, lanes], sums_in.at[2, low_rows, lanes], depth[6])
     ahead = terms[2]
     terms = share(BATCHES[1])
     behind = terms[6]
@@ -315,18 +333,18 @@
         summed, peak, total = terms[o]
         sums[o] = summed.astype(BF16)
         stats[o] = stat_block(peak, total)
-    arrivals["stat1"] = send(8, stats.at[1], stats_in.at[4], depth[1])
-    arrivals["stat7"] = send(9, stats.at[7], stats_in.at[5], depth[7])
-    arrivals["sum1"] = send(10, sums.at[1], sums_in.at[3], depth[1])
-    arrivals["sum7"] = send(11, sums.at[7], sums_in.at[4], depth[7])
+    arrivals["stat1"] = send(4, stats.at[1], stats_in.at[4], depth[1])
+    arrivals["stat7"] = send(5, stats.at[7], stats_in.at[5], depth[7])
+    arrivals["sum1"] = send(32, sums.at[1], sums_in.at[3], depth[1])
+    arrivals["sum7"] = send(33, sums.at[7], sums_in.at[4], depth[7])
     own_sum, own_peak, own_total = terms[0]
 
     def columns(blocks):
         filled = jnp.concatenate(blocks + [jnp.zeros((128 - 8 * len(blocks), 128), F32)], axis=0)
         return jnp.transpose(filled)[0:64, :]
 
-    def relay(own, full, half, first_rows):
-        own_sum, own_peak, own_total = own
+    def relay_scales(own, full, half, first_rows):
+        _, own_peak, own_total = own
         arrivals["stat3" if first_rows else "stat5"].wait_recv()
         arrivals["stat4" if first_rows else "stat4b"].wait_recv()
         spread = columns([stats_in[full], stats_in[half]])
@@ -341,22 +359,31 @@
         full_scale = jnp.exp(full_peak - peak)
         half_scale = jnp.exp(half_peak - peak)
         total = own_scale * own_total + full_scale * spread[:, 1:2] + half_scale * half_total
-        arrivals["sum3" if first_rows else "sum5"].wait_recv()
-        merged = own_scale * own_sum + full_scale * sums_in[full].astype(F32)
-        arrivals["sum4" if first_rows else "sum4b"].wait_recv()
-        rows = slice(0, 32) if first_rows else slice(32, 64)
-        extra = half_scale[rows] * sums_in[2, rows, :].astype(F32)
-        pieces = [merged[0:32], merged[32:64]]
-        pieces[0 if first_rows else 1] = pieces[0 if first_rows else 1] + extra
-        return jnp.concatenate(pieces, axis=0), peak, total
-
-    for n, (own, full, half, first_rows) in enumerate(((ahead, 0, 2, True), (behind, 1, 3, False))):
-        summed, peak, total = relay(own, full, half, first_rows)
-        o = 2 if first_rows else 6
+        return peak, total, own_scale, full_scale, half_scale
+
+    routes = ((ahead, 0, 2, True), (behind, 1, 3, False))
+    route_scales = []
+    for n, route in enumerate(routes):
+        peak, total, *rest = relay_scales(*route)
+        route_scales.append(rest)
+        o = 2 if route[3] else 6
         stats[o] = stat_block(peak, total)
-        arrivals["stat%d" % o] = send(12 + n, stats.at[o], stats_in.at[6 + n], depth[o])
-        sums[o] = summed.astype(BF16)
-        arrivals["sum%d" % o] = send(14 + n, sums.at[o], sums_in.at[5 + n], depth[o])
+        arrivals["stat%d" % o] = send(6 + n, stats.at[o], stats_in.at[6 + n], depth[o])
+    for h, lanes in enumerate(HALVES):
+        cut = slice(lanes.start, lanes.start + lanes.size)
+        for n, (own, full, half, first_rows) in enumerate(routes):
+            own_scale, full_scale, half_scale = route_scales[n]
+            arrivals["sum3" if first_rows else "sum5", h].wait_recv()
+            merged = own_scale * own[0][:, cut] + full_scale * sums_in[full, :, cut].astype(F32)
+            arrivals["sum4" if first_rows else "sum4b", h].wait_recv()
+            rows = slice(0, 32) if first_rows else slice(32, 64)
+            extra = half_scale[rows] * sums_in[2, rows, cut].astype(F32)
+            pieces = [merged[0:32], merged[32:64]]
+            k = 0 if first_rows else 1
+            pieces[k] = pieces[k] + extra
+            o = 2 if first_rows else 6
+            sums[o, :, cut] = jnp.concatenate(pieces, axis=0).astype(BF16)
+            arrivals["sum%d" % o, h] = send(24 + 4 * n + h, sums.at[o, :, lanes], sums_in.at[5 + n, :, lanes], depth[o])
 
     for name in ("stat1", "stat7", "stat2", "stat6"):
         arrivals[name].wait_recv()
@@ -373,10 +400,17 @@
     for scale, total in zip(scales, totals):
         denominator = denominator + scale * total
     numerator = fresh_scale * fresh_sum + own_scale * own_sum
-    for k, name in enumerate(("sum1", "sum7", "sum2", "sum6")):
+    for k, name in enumerate(("sum1", "sum7")):
         arrivals[name].wait_recv()
         numerator = numerator + scales[k] * sums_in[3 + k].astype(F32)
-    out[...] = (numerator / denominator).astype(BF16).reshape(2, 1, 2, 16, LAT)
+    inverse = 1.0 / denominator
+    for h, lanes in enumerate(HALVES):
+        cut = slice(lanes.start, lanes.start + lanes.size)
+        piece = numerator[:, cut]
+        for n, name in enumerate(("sum2", "sum6")):
+            arrivals[name, h].wait_recv()
+            piece = piece + scales[2 + n] * sums_in[5 + n, :, cut].astype(F32)
+        out[:, :, :, :, cut] = (piece * inverse).astype(BF16).reshape(2, 1, 2, 16, lanes.size)
 
     for copy in s1 + qc + s2 + s3 + s4:
         copy.wait_send()
@@ -386,7 +420,8 @@
     vmem = pl.BlockSpec(memory_space=pltpu.VMEM)
     hbm = pl.BlockSpec(memory_space=pltpu.HBM)
     dma = pltpu.SemaphoreType.DMA
-    blocks = [pltpu.VMEM((8, 64, width), BF16) for width in WIDTHS]
+    chunks = len(CHUNKS)
+    blocks = [pltpu.VMEM((8, 64, width), BF16) for _, width in CHUNKS]
     return pl.pallas_call(
         kernel,
         out_shape=(
@@ -407,13 +442,13 @@
             pltpu.VMEM((8, 16, 384), BF16),
             pltpu.VMEM((8, 2, 2, 16, LATW), BF16),
             pltpu.VMEM((512, 512), BF16),
-            *blocks, *blocks, *blocks,
             pltpu.VMEM((8, 64, LAT), BF16),
             pltpu.VMEM((8, 64, LAT), BF16),
             pltpu.VMEM((8, 8, 128), F32),
             pltpu.VMEM((8, 8, 128), F32),
-            dma((8,)), dma((7,)), dma((7,)), dma((3, 8)), dma((3, 8)),
-            dma((3, 8)), dma((3, 8)), dma((7,)), dma((7,)), dma((16,)), dma((16,)),
+            dma((8,)), dma((7,)), dma((7,)), dma((chunks, 8)), dma((chunks, 8)),
+            dma((chunks, 8)), dma((chunks, 8)), dma((7,)), dma((7,)), dma((34,)), dma((34,)),
+            *blocks, *blocks, *blocks,
         ],
         compiler_params=pltpu.CompilerParams(
             collective_id=0, has_side_effects=True, vmem_limit_bytes=24 * 1024 * 1024

time: 51 us -> 49.9 us (0.978)
  the two profiles are of different devices: /device:TPU:2 before, /device:TPU:1 now
where the time goes in v4:
time: 49.9 us; the launch traced here: 49.8 us
  Pallas kernels  47.9 us (96%)
  local copies, waits for them, and re-layouts  1.27 us (3%)
  between operations  0.64 us (1%)
    pallas_call x1, Pallas kernels, local(): pl.pallas_call(kernel, out_shape=(jax.ShapeDtypeStruct((2, 1, 2, 16, LAT)...  47.9 us
    unnamed x2, local copies, waits for them, and re-layouts  1.27 us

profile of v4, /device:TPU:1, one launch (start us, length us, event | category | flops | bytes accessed | tf_op | source)
XLA Modules:
  0.0 49.8 jit_solution(6689079141334401353)
XLA Ops:
  0.6 47.9 %place_and_attend.1 = (bf16[2,1,2,16,512]{4,3,2,1,0:T(8,128)(2,1)S(1)}, bf16[8,8,576]{2,1,0:T(8,128)(2,1)S(1)}) custom-call(bf16[8,64,576]{2,1,0:T(8,128)(2,1)} %prefill_hbm.1, s32[512]{0:T(512)} %stretch_hbm.1, s32[1,512]{1,0:T(1,128)} %bitcast.2, s32[2,512]{1,0:T(2,128)} %bitcast.3, s32[64,64]{1,0:T(8,128)} %plist_hbm.1, s32[64]{0:T(128)} %lengths_hbm.1, ...), custom_call_target="tpu_custom_call" | custom-call | tf_op jit(solution)/shard_map/place_and_attend/pallas_call | solution.py:425
  48.5 0.6 %copy.11 = bf16[2,1,2,16,512]{4,3,2,1,0:T(8,128)(2,1)} copy(bf16[2,1,2,16,512]{4,3,2,1,0:T(8,128)(2,1)S(1)} %get-tuple-element.4) | data formatting | bytes 131072
  49.2 0.6 %copy.12 = bf16[8,8,576]{2,1,0:T(8,128)(2,1)} copy(bf16[8,8,576]{2,1,0:T(8,128)(2,1)S(1)} %get-tuple-element.5) | data formatting | bytes 147456

commit v5 on v4

--- a/solution.py
+++ b/solution.py
@@ -59,7 +59,7 @@
     outgoing, incoming, all_queries, picks,
     sums, sums_in, stats, stats_in,
     load_sem, s1_send, s1_recv, s2_send, s2_recv,
-    s3_send, s3_recv, q_send, q_recv, s4_send, s4_recv, *blocks,
+    s3_send, s3_recv, q_send, q_recv, s4_send, s4_recv, st_send, *blocks,
 ):
     chunks = len(CHUNKS)
     gathered, picked, keys = blocks[:chunks], blocks[chunks : 2 * chunks], blocks[2 * chunks :]
@@ -101,6 +101,9 @@
     targets += [in_depth(i) for i in depth_peers]
     for target in targets:
         pl.semaphore_signal(barrier, inc=1, device_id=target, device_id_type=pl.DeviceIdType.MESH)
+
+    def drain(ref, sem):
+        pltpu.make_async_copy(ref, ref, sem).wait()
 
     def remote(src, dst, send, recv, target):
         return pltpu.make_async_remote_copy(
@@ -128,55 +131,40 @@
 
     pl.semaphore_wait(barrier, len(targets))
 
-    s1 = []
-    for n, i in enumerate(row_peers):
-        copy = remote(outgoing.at[i], incoming.at[q], s1_send.at[n], s1_recv.at[n], in_row(i))
+    for i in row_peers:
+        copy = remote(outgoing.at[i], incoming.at[q], s1_send, s1_recv, in_row(i))
         copy.start()
-        s1.append(copy)
     incoming[q] = outgoing[q]
 
     for copy in loads[3:]:
         copy.wait()
-    qc = []
-    for n, i in enumerate(depth_peers):
-        copy = remote(all_queries.at[z], all_queries.at[z], q_send.at[n], q_recv.at[n], in_depth(i))
-        copy.start()
-        qc.append(copy)
-    for copy in s1:
-        copy.wait_recv()
+    for i in depth_peers:
+        remote(all_queries.at[z], all_queries.at[z], q_send, q_recv, in_depth(i)).start()
+    drain(incoming.at[pl.ds(0, 7)], s1_recv)
     arrived = incoming[...].astype(F32)
     whole = jnp.concatenate([arrived[:, 0:8, 0:256], arrived[:, 8:16, 0:256], arrived[:, 0:8, 256:384]], axis=2)
     whole = whole.reshape(64, WIDE).astype(BF16)
     for c, (start, width) in enumerate(CHUNKS):
         gathered[c][y] = whole[:, start : start + width]
 
-    s2 = []
 
     def along(c, kind, block, rows, step):
         view = gathered[c].at[lax.rem(block + NY, NY), pl.ds(rows[0], rows[1]), :]
-        copy = remote(view, view, s2_send.at[c, kind], s2_recv.at[c, kind], in_column(step))
-        copy.start()
-        s2.append(copy)
-        return copy
-
-    near = []
-    far = []
+        remote(view, view, s2_send.at[c], s2_recv.at[c, min(kind, 2)], in_column(step)).start()
 
     def start_near(c):
-        near.append([
-            along(c, 0, y, (0, 64), 2),
-            along(c, 1, y, (0, 64), -2),
-            along(c, 2, y, (0, 64), 1),
-            along(c, 3, y, (0, 64), -1),
-        ])
+        along(c, 0, y, (0, 64), 2)
+        along(c, 1, y, (0, 64), -2)
+        along(c, 2, y, (0, 64), 1)
+        along(c, 3, y, (0, 64), -1)
 
     def start_far(c):
-        near[c][0].wait_recv()
-        below = [along(c, 4, y - 2, (0, 64), 1), along(c, 6, y - 2, (0, 32), 2)]
-        near[c][1].wait_recv()
-        far.append(below + [along(c, 5, y + 2, (0, 64), -1), along(c, 7, y + 2, (32, 32), -2)])
-
-    s3 = []
+        drain(gathered[c].at[0], s2_recv.at[c, 0])
+        along(c, 4, y - 2, (0, 64), 1)
+        along(c, 6, y - 2, (0, 32), 2)
+        drain(gathered[c].at[0], s2_recv.at[c, 1])
+        along(c, 5, y + 2, (0, 64), -1)
+        along(c, 7, y + 2, (32, 32), -2)
 
     def part(ref, i, c):
         return ref[c].at[i]
@@ -184,29 +172,27 @@
     def hand(c, m, parity):
         i = lax.rem(q // 2 + m, 4) * 2 + parity
         copy = remote(
-            part(picked, i, c), part(keys, q, c), s3_send.at[c, m * 2 + parity], s3_recv.at[c, m * 2 + core], in_row(i)
+            part(picked, i, c), part(keys, q, c), s3_send.at[c], s3_recv.at[c], in_row(i)
         )
         copy.start()
-        s3.append(copy)
 
     def hand_sibling(c):
         i = q + 1 - 2 * core
-        copy = remote(part(picked, i, c), part(keys, q, c), s3_send.at[c, 0], s3_recv.at[c, 0], in_row(i))
+        copy = remote(part(picked, i, c), part(keys, q, c), s3_send.at[c], s3_recv.at[c], in_row(i))
         copy.start()
-        s3.append(copy)
 
     def hand_core(c, parity):
         for m in (2, 1, 3):
             hand(c, m, parity)
 
     def pass_on(c):
-        for copy in near[c][2:] + far[c]:
-            copy.wait_recv()
+        drain(gathered[c].at[pl.ds(0, 5)], s2_recv.at[c, 2])
         width = CHUNKS[c][1]
         have = gathered[c][...].reshape(512, width)
         picked[c][...] = dot(picks[...], have).astype(BF16).reshape(8, 64, width)
-        hand_core(c, 0)
-        hand_core(c, 1)
+        for m in (2, 1, 3):
+            hand(c, m, 0)
+            hand(c, m, 1)
         hand_sibling(c)
         keys[c][q] = picked[c][q]
 
@@ -264,30 +250,19 @@
     position = ((token // 64 - shift - begin) & 7) + 8 * ((token & 63) // 8)
     live = position * PAGE + z * SHARE + (token & 7) < lengths[p]
 
-    for copy in qc:
-        copy.wait_recv()
-    for c in range(len(CHUNKS)):
-        for n in range(8):
-            if n == 1:
-                continue
-            if n == 0:
-                source = q + 1 - 2 * core
-            else:
-                source = lax.rem(q // 2 + 4 - n // 2, 4) * 2 + n % 2
-            remote(
-                part(picked, source, c), part(keys, source, c), s3_send.at[c, n], s3_recv.at[c, n], in_row(source)
-            ).wait_recv()
+    drain(all_queries.at[pl.ds(0, 7)], q_recv)
+    for c in range(chunks):
+        drain(keys[c].at[pl.ds(0, 7)], s3_recv.at[c])
     latents = joined(keys)
     narrow = latents[:, 0:LATW]
     values = latents[:, 0:LAT]
 
-    s4 = []
-
-    def send(n, src, dst, target):
-        copy = remote(src, dst, s4_send.at[n], s4_recv.at[n], in_depth(target))
-        copy.start()
-        s4.append(copy)
-        return copy
+
+    def send(src, dst, sem, target):
+        remote(src, dst, s4_send, s4_recv.at[sem], in_depth(target)).start()
+
+    def send_stat(src, dst, sem, target):
+        remote(stats.at[src], stats_in.at[dst], st_send, s4_recv.at[sem], in_depth(target)).start()
 
     def stat_block(peak, total):
         lane = iota((64, 128), 1)
@@ -310,22 +285,21 @@
         return terms
 
     depth = [lax.rem(z + o, NZ) for o in range(NZ)]
-    arrivals = {}
     terms = share(BATCHES[0])
     for o in (3, 5, 4):
         summed, peak, total = terms[o]
         sums[o] = summed.astype(BF16)
         stats[o] = stat_block(peak, total)
-    arrivals["stat3"] = send(0, stats.at[3], stats_in.at[0], depth[1])
-    arrivals["stat5"] = send(1, stats.at[5], stats_in.at[1], depth[7])
-    arrivals["stat4"] = send(2, stats.at[4], stats_in.at[2], depth[2])
-    arrivals["stat4b"] = send(3, stats.at[4], stats_in.at[3], depth[6])
+    send_stat(3, 0, 0, depth[1])
+    send_stat(5, 1, 0, depth[7])
+    send_stat(4, 2, 0, depth[2])
+    send_stat(4, 3, 0, depth[6])
+    top_rows, low_rows = pl.ds(0, 32), pl.ds(32, 32)
     for h, lanes in enumerate(HALVES):
-        arrivals["sum3", h] = send(8 + h, sums.at[3, :, lanes], sums_in.at[0, :, lanes], depth[1])
-        arrivals["sum5", h] = send(12 + h, sums.at[5, :, lanes], sums_in.at[1, :, lanes], depth[7])
-        top_rows, low_rows = pl.ds(0, 32), pl.ds(32, 32)
-        arrivals["sum4", h] = send(16 + h, sums.at[4, top_rows, lanes], sums_in.at[2, top_rows, lanes], depth[2])
-        arrivals["sum4b", h] = send(20 + h, sums.at[4, low_rows, lanes], sums_in.at[2, low_rows, lanes], depth[6])
+        send(sums.at[3, :, lanes], sums_in.at[0, :, lanes], 2 + h, depth[1])
+        send(sums.at[5, :, lanes], sums_in.at[1, :, lanes], 2 + h, depth[7])
+        send(sums.at[4, top_rows, lanes], sums_in.at[2, top_rows, lanes], 2 + h, depth[2])
+        send(sums.at[4, low_rows, lanes], sums_in.at[2, low_rows, lanes], 2 + h, depth[6])
     ahead = terms[2]
     terms = share(BATCHES[1])
     behind = terms[6]
@@ -333,10 +307,10 @@
         summed, peak, total = terms[o]
         sums[o] = summed.astype(BF16)
         stats[o] = stat_block(peak, total)
-    arrivals["stat1"] = send(4, stats.at[1], stats_in.at[4], depth[1])
-    arrivals["stat7"] = send(5, stats.at[7], stats_in.at[5], depth[7])
-    arrivals["sum1"] = send(32, sums.at[1], sums_in.at[3], depth[1])
-    arrivals["sum7"] = send(33, sums.at[7], sums_in.at[4], depth[7])
+    send_stat(1, 4, 1, depth[1])
+    send_stat(7, 5, 1, depth[7])
+    send(sums.at[1], sums_in.at[3], 4, depth[1])
+    send(sums.at[7], sums_in.at[4], 4, depth[7])
     own_sum, own_peak, own_total = terms[0]
 
     def columns(blocks):
@@ -345,8 +319,6 @@
 
     def relay_scales(own, full, half, first_rows):
         _, own_peak, own_total = own
-        arrivals["stat3" if first_rows else "stat5"].wait_recv()
-        arrivals["stat4" if first_rows else "stat4b"].wait_recv()
         spread = columns([stats_in[full], stats_in[half]])
         inside = iota((64, 1), 0) < 32
         if not first_rows:
@@ -363,19 +335,19 @@
 
     routes = ((ahead, 0, 2, True), (behind, 1, 3, False))
     route_scales = []
+    drain(stats_in.at[pl.ds(0, 4)], s4_recv.at[0])
     for n, route in enumerate(routes):
         peak, total, *rest = relay_scales(*route)
         route_scales.append(rest)
         o = 2 if route[3] else 6
         stats[o] = stat_block(peak, total)
-        arrivals["stat%d" % o] = send(6 + n, stats.at[o], stats_in.at[6 + n], depth[o])
+        send_stat(o, 6 + n, 1, depth[o])
     for h, lanes in enumerate(HALVES):
         cut = slice(lanes.start, lanes.start + lanes.size)
+        drain(sums_in.at[pl.ds(0, 3), :, lanes], s4_recv.at[2 + h])
         for n, (own, full, half, first_rows) in enumerate(routes):
             own_scale, full_scale, half_scale = route_scales[n]
-            arrivals["sum3" if first_rows else "sum5", h].wait_recv()
             merged = own_scale * own[0][:, cut] + full_scale * sums_in[full, :, cut].astype(F32)
-            arrivals["sum4" if first_rows else "sum4b", h].wait_recv()
             rows = slice(0, 32) if first_rows else slice(32, 64)
             extra = half_scale[rows] * sums_in[2, rows, cut].astype(F32)
             pieces = [merged[0:32], merged[32:64]]
@@ -383,10 +355,9 @@
             pieces[k] = pieces[k] + extra
             o = 2 if first_rows else 6
             sums[o, :, cut] = jnp.concatenate(pieces, axis=0).astype(BF16)
-            arrivals["sum%d" % o, h] = send(24 + 4 * n + h, sums.at[o, :, lanes], sums_in.at[5 + n, :, lanes], depth[o])
-
-    for name in ("stat1", "stat7", "stat2", "stat6"):
-        arrivals[name].wait_recv()
+            send(sums.at[o, :, lanes], sums_in.at[5 + n, :, lanes], 5 + h, depth[o])
+
+    drain(stats_in.at[pl.ds(4, 4)], s4_recv.at[1])
     spread = columns([stats_in[k] for k in (4, 5, 6, 7)])
     peaks = [spread[:, 8 * k : 8 * k + 1] for k in range(4)]
     totals = [spread[:, 8 * k + 1 : 8 * k + 2] for k in range(4)]
@@ -400,20 +371,25 @@
     for scale, total in zip(scales, totals):
         denominator = denominator + scale * total
     numerator = fresh_scale * fresh_sum + own_scale * own_sum
-    for k, name in enumerate(("sum1", "sum7")):
-        arrivals[name].wait_recv()
+    drain(sums_in.at[pl.ds(3, 2)], s4_recv.at[4])
+    for k in range(2):
         numerator = numerator + scales[k] * sums_in[3 + k].astype(F32)
     inverse = 1.0 / denominator
     for h, lanes in enumerate(HALVES):
         cut = slice(lanes.start, lanes.start + lanes.size)
         piece = numerator[:, cut]
-        for n, name in enumerate(("sum2", "sum6")):
-            arrivals[name, h].wait_recv()
+        drain(sums_in.at[pl.ds(5, 2), :, lanes], s4_recv.at[5 + h])
+        for n in range(2):
             piece = piece + scales[2 + n] * sums_in[5 + n, :, cut].astype(F32)
         out[:, :, :, :, cut] = (piece * inverse).astype(BF16).reshape(2, 1, 2, 16, lanes.size)
 
-    for copy in s1 + qc + s2 + s3 + s4:
-        copy.wait_send()
+    drain(outgoing.at[pl.ds(0, 7)], s1_send)
+    drain(all_queries.at[pl.ds(0, 7)], q_send)
+    for c in range(chunks):
+        drain(gathered[c].at[pl.ds(0, 7)], s2_send.at[c])
+        drain(picked[c].at[pl.ds(0, 7)], s3_send.at[c])
+    drain(stats, st_send)
+    drain(sums.at[pl.ds(0, 7)], s4_send)
 
 
 def local(prefill_latent, stretch_page, page_table, page_list, lengths, queries, new_latent):
@@ -446,8 +422,8 @@
             pltpu.VMEM((8, 64, LAT), BF16),
             pltpu.VMEM((8, 8, 128), F32),
             pltpu.VMEM((8, 8, 128), F32),
-            dma((8,)), dma((7,)), dma((7,)), dma((chunks, 8)), dma((chunks, 8)),
-            dma((chunks, 8)), dma((chunks, 8)), dma((7,)), dma((7,)), dma((34,)), dma((34,)),
+            dma((8,)), dma, dma, dma((chunks,)), dma((chunks, 3)),
+            dma((chunks,)), dma((chunks,)), dma, dma, dma, dma((7,)), dma,
             *blocks, *blocks, *blocks,
         ],
         compiler_params=pltpu.CompilerParams(

time: 49.9 us -> 48.2 us (0.966)
  Pallas kernels: 47.9 us -> 45.9 us
    pallas_call x1, Pallas kernels: 47.9 us -> 45.9 us  [local(): pl.pallas_call(kernel, out_shape=(jax.ShapeDtypeStruct((2, 1, 2, 16, LAT)...]
where the time goes in v5:
time: 48.2 us; the launch traced here: 47.8 us
  Pallas kernels  45.9 us (95%)
  local copies, waits for them, and re-layouts  1.27 us (3%)
  between operations  0.64 us (1%)
    pallas_call x1, Pallas kernels, local(): pl.pallas_call(kernel, out_shape=(jax.ShapeDtypeStruct((2, 1, 2, 16, LAT)...  45.9 us
    unnamed x2, local copies, waits for them, and re-layouts  1.27 us

profile of v5, /device:TPU:1, one launch (start us, length us, event | category | flops | bytes accessed | tf_op | source)
XLA Modules:
  0.0 47.8 jit_solution(8429865997856111970)
XLA Ops:
  0.6 45.9 %place_and_attend.1 = (bf16[2,1,2,16,512]{4,3,2,1,0:T(8,128)(2,1)S(1)}, bf16[8,8,576]{2,1,0:T(8,128)(2,1)S(1)}) custom-call(bf16[8,64,576]{2,1,0:T(8,128)(2,1)} %prefill_hbm.1, s32[512]{0:T(512)} %stretch_hbm.1, s32[1,512]{1,0:T(1,128)} %bitcast.2, s32[2,512]{1,0:T(2,128)} %bitcast.3, s32[64,64]{1,0:T(8,128)} %plist_hbm.1, s32[64]{0:T(128)} %lengths_hbm.1, ...), custom_call_target="tpu_custom_call" | custom-call | tf_op jit(solution)/shard_map/place_and_attend/pallas_call | solution.py:401
  46.5 0.6 %copy.11 = bf16[2,1,2,16,512]{4,3,2,1,0:T(8,128)(2,1)} copy(bf16[2,1,2,16,512]{4,3,2,1,0:T(8,128)(2,1)S(1)} %get-tuple-element.4) | data formatting | bytes 131072
  47.2 0.6 %copy.12 = bf16[8,8,576]{2,1,0:T(8,128)(2,1)} copy(bf16[8,8,576]{2,1,0:T(8,128)(2,1)S(1)} %get-tuple-element.5) | data formatting | bytes 147456

commit v6 on v5

--- a/solution.py
+++ b/solution.py
@@ -13,23 +13,26 @@
 NZ = 8
 SHARE = 8
 WIDE = 640
-CHUNKS = ((512, 128), (0, 256), (256, 256))
+CHUNKS = ((512, 128), (0, 128), (128, 256), (384, 128))
 SOFTMAX_SCALE = 192.0 ** (-0.5)
 MASKED_SCORE = -1e30
 F32 = jnp.float32
 BF16 = jnp.bfloat16
 I32 = jnp.int32
-FIRST = 2
+FIRST = 3
 ORDER = (
     ("near", 0),
     ("near", 1),
+    ("near", 2),
     ("far", 0),
-    ("near", 2),
     ("far", 1),
+    ("near", 3),
+    ("far", 2),
     ("pass", 0),
-    ("far", 2),
     ("pass", 1),
+    ("far", 3),
     ("pass", 2),
+    ("pass", 3),
 )
 HALVES = (pl.ds(0, 256), pl.ds(256, 256))
 DEPTH_ORDER = (4, 3, 5, 2, 6, 1, 7)
@@ -264,36 +267,38 @@
     def send_stat(src, dst, sem, target):
         remote(stats.at[src], stats_in.at[dst], st_send, s4_recv.at[sem], in_depth(target)).start()
 
-    def stat_block(peak, total):
+    def stat_rows(pairs):
         lane = iota((64, 128), 1)
-        block = jnp.transpose(jnp.where(lane == 0, peak, jnp.where(lane == 1, total, 0.0)))[0:8, :]
-        return jnp.concatenate([block, block], axis=1)
-
-    def share(offsets):
+        block = jnp.zeros((64, 128), F32)
+        for k, (peak, total) in enumerate(pairs):
+            block = jnp.where(lane == 8 * k, peak, jnp.where(lane == 8 * k + 1, total, block))
+        rows = jnp.transpose(block)
+        return [jnp.concatenate([rows[8 * k : 8 * k + 8]] * 2, axis=1) for k in range(len(pairs))]
+
+    def weigh(offsets):
         asked = jnp.concatenate([all_queries[depth[o]].reshape(64, LATW) for o in offsets], axis=0)
         scores = dot_last(asked, narrow) * SOFTMAX_SCALE
         scores = jnp.where(live, scores, MASKED_SCORE)
         peak = jnp.max(scores, axis=1, keepdims=True)
         weight = jnp.where(live, jnp.exp(scores - peak), 0.0)
         total = jnp.sum(weight, axis=1, keepdims=True)
-        weight = weight.astype(BF16)
+        pairs = {o: (peak[64 * k : 64 * k + 64], total[64 * k : 64 * k + 64]) for k, o in enumerate(offsets)}
+        return weight.astype(BF16), pairs
+
+    def add_up(offsets, weight, pairs):
         summed = dot(weight, values)
-        terms = {}
-        for k, o in enumerate(offsets):
-            rows = slice(64 * k, 64 * k + 64)
-            terms[o] = (summed[rows], peak[rows], total[rows])
-        return terms
+        return {o: (summed[64 * k : 64 * k + 64],) + pairs[o] for k, o in enumerate(offsets)}
 
     depth = [lax.rem(z + o, NZ) for o in range(NZ)]
-    terms = share(BATCHES[0])
+    weight, pairs = weigh(BATCHES[0])
+    stats[3], stats[5], stats[4] = stat_rows([pairs[o] for o in (3, 5, 4)])
+    send_stat(3, 0, 0, depth[1])
+    send_stat(5, 2, 0, depth[7])
+    send_stat(4, 1, 0, depth[2])
+    send_stat(4, 3, 0, depth[6])
+    terms = add_up(BATCHES[0], weight, pairs)
     for o in (3, 5, 4):
-        summed, peak, total = terms[o]
-        sums[o] = summed.astype(BF16)
-        stats[o] = stat_block(peak, total)
-    send_stat(3, 0, 0, depth[1])
-    send_stat(5, 1, 0, depth[7])
-    send_stat(4, 2, 0, depth[2])
-    send_stat(4, 3, 0, depth[6])
+        sums[o] = terms[o][0].astype(BF16)
     top_rows, low_rows = pl.ds(0, 32), pl.ds(32, 32)
     for h, lanes in enumerate(HALVES):
         send(sums.at[3, :, lanes], sums_in.at[0, :, lanes], 2 + h, depth[1])
@@ -301,14 +306,14 @@
         send(sums.at[4, top_rows, lanes], sums_in.at[2, top_rows, lanes], 2 + h, depth[2])
         send(sums.at[4, low_rows, lanes], sums_in.at[2, low_rows, lanes], 2 + h, depth[6])
     ahead = terms[2]
-    terms = share(BATCHES[1])
+    weight, pairs = weigh(BATCHES[1])
+    stats[1], stats[7] = stat_rows([pairs[o] for o in (1, 7)])
+    send_stat(1, 4, 1, depth[1])
+    send_stat(7, 5, 1, depth[7])
+    terms = add_up(BATCHES[1], weight, pairs)
     behind = terms[6]
     for o in (1, 7):
-        summed, peak, total = terms[o]
-        sums[o] = summed.astype(BF16)
-        stats[o] = stat_block(peak, total)
-    send_stat(1, 4, 1, depth[1])
-    send_stat(7, 5, 1, depth[7])
+        sums[o] = terms[o][0].astype(BF16)
     send(sums.at[1], sums_in.at[3], 4, depth[1])
     send(sums.at[7], sums_in.at[4], 4, depth[7])
     own_sum, own_peak, own_total = terms[0]
@@ -317,35 +322,32 @@
         filled = jnp.concatenate(blocks + [jnp.zeros((128 - 8 * len(blocks), 128), F32)], axis=0)
         return jnp.transpose(filled)[0:64, :]
 
-    def relay_scales(own, full, half, first_rows):
+    def relay_scales(n, own, first_rows):
         _, own_peak, own_total = own
-        spread = columns([stats_in[full], stats_in[half]])
         inside = iota((64, 1), 0) < 32
         if not first_rows:
             inside = jnp.logical_not(inside)
-        full_peak = spread[:, 0:1]
-        half_peak = jnp.where(inside, spread[:, 8:9], MASKED_SCORE)
-        half_total = jnp.where(inside, spread[:, 9:10], 0.0)
+        full_peak, full_total, half_peak, half_total = [spread[:, 16 * n + k : 16 * n + k + 1] for k in (0, 1, 8, 9)]
+        half_peak = jnp.where(inside, half_peak, MASKED_SCORE)
+        half_total = jnp.where(inside, half_total, 0.0)
         peak = jnp.maximum(jnp.maximum(own_peak, full_peak), half_peak)
         own_scale = jnp.exp(own_peak - peak)
         full_scale = jnp.exp(full_peak - peak)
         half_scale = jnp.exp(half_peak - peak)
-        total = own_scale * own_total + full_scale * spread[:, 1:2] + half_scale * half_total
-        return peak, total, own_scale, full_scale, half_scale
-
-    routes = ((ahead, 0, 2, True), (behind, 1, 3, False))
-    route_scales = []
+        total = own_scale * own_total + full_scale * full_total + half_scale * half_total
+        return (peak, total), (own_scale, full_scale, half_scale)
+
+    routes = ((ahead, 0, True), (behind, 1, False))
     drain(stats_in.at[pl.ds(0, 4)], s4_recv.at[0])
-    for n, route in enumerate(routes):
-        peak, total, *rest = relay_scales(*route)
-        route_scales.append(rest)
-        o = 2 if route[3] else 6
-        stats[o] = stat_block(peak, total)
-        send_stat(o, 6 + n, 1, depth[o])
+    spread = columns([stats_in[k] for k in range(4)])
+    merged_pairs, route_scales = zip(*[relay_scales(n, own, first_rows) for n, (own, _, first_rows) in enumerate(routes)])
+    stats[2], stats[6] = stat_rows(merged_pairs)
+    send_stat(2, 6, 1, depth[2])
+    send_stat(6, 7, 1, depth[6])
     for h, lanes in enumerate(HALVES):
         cut = slice(lanes.start, lanes.start + lanes.size)
         drain(sums_in.at[pl.ds(0, 3), :, lanes], s4_recv.at[2 + h])
-        for n, (own, full, half, first_rows) in enumerate(routes):
+        for n, (own, full, first_rows) in enumerate(routes):
             own_scale, full_scale, half_scale = route_scales[n]
             merged = own_scale * own[0][:, cut] + full_scale * sums_in[full, :, cut].astype(F32)
             rows = slice(0, 32) if first_rows else slice(32, 64)

time: 48.2 us -> 47.7 us (0.990)
  no operation moved by 1% of the time
where the time goes in v6:
time: 47.7 us; the launch traced here: 47.5 us
  Pallas kernels  45.6 us (96%)
  local copies, waits for them, and re-layouts  1.27 us (3%)
  between operations  0.64 us (1%)
    pallas_call x1, Pallas kernels, local(): pl.pallas_call(kernel, out_shape=(jax.ShapeDtypeStruct((2, 1, 2, 16, LAT)...  45.6 us
    unnamed x2, local copies, waits for them, and re-layouts  1.27 us

profile of v6, /device:TPU:1, one launch (start us, length us, event | category | flops | bytes accessed | tf_op | source)
XLA Modules:
  0.0 47.5 jit_solution(1834226436968887563)
XLA Ops:
  0.6 45.6 %place_and_attend.1 = (bf16[2,1,2,16,512]{4,3,2,1,0:T(8,128)(2,1)S(1)}, bf16[8,8,576]{2,1,0:T(8,128)(2,1)S(1)}) custom-call(bf16[8,64,576]{2,1,0:T(8,128)(2,1)} %prefill_hbm.1, s32[512]{0:T(512)} %stretch_hbm.1, s32[1,512]{1,0:T(1,128)} %bitcast.2, s32[2,512]{1,0:T(2,128)} %bitcast.3, s32[64,64]{1,0:T(8,128)} %plist_hbm.1, s32[64]{0:T(128)} %lengths_hbm.1, ...), custom_call_target="tpu_custom_call" | custom-call | tf_op jit(solution)/shard_map/place_and_attend/pallas_call | solution.py:403
  46.2 0.6 %copy.11 = bf16[2,1,2,16,512]{4,3,2,1,0:T(8,128)(2,1)} copy(bf16[2,1,2,16,512]{4,3,2,1,0:T(8,128)(2,1)S(1)} %get-tuple-element.4) | data formatting | bytes 131072
  46.8 0.6 %copy.12 = bf16[8,8,576]{2,1,0:T(8,128)(2,1)} copy(bf16[8,8,576]{2,1,0:T(8,128)(2,1)S(1)} %get-tuple-element.5) | data formatting | bytes 147456

commit v7 on v6

--- a/solution.py
+++ b/solution.py
@@ -98,7 +98,7 @@
         loads.append(copy)
 
     barrier = pltpu.get_barrier_semaphore()
-    row_peers = [lax.rem(q + o, NQ) for o in range(1, NQ)]
+    row_peers = [lax.rem(q + o, NQ) for o in (4, 3, 5, 2, 6, 1, 7)]
     depth_peers = [lax.rem(z + o, NZ) for o in DEPTH_ORDER]
     targets = [in_row(i) for i in row_peers] + [in_column(d) for d in (1, -1, 2, -2)]
     targets += [in_depth(i) for i in depth_peers]

time: 47.7 us -> 47.6 us (level)
  no operation moved by 1% of the time
where the time goes in v7:
time: 47.6 us; the launch traced here: 47.5 us
  Pallas kernels  45.6 us (96%)
  local copies, waits for them, and re-layouts  1.27 us (3%)
  between operations  0.64 us (1%)
    pallas_call x1, Pallas kernels, local(): pl.pallas_call(kernel, out_shape=(jax.ShapeDtypeStruct((2, 1, 2, 16, LAT)...  45.6 us
    unnamed x2, local copies, waits for them, and re-layouts  1.27 us

profile of v7, /device:TPU:1, one launch (start us, length us, event | category | flops | bytes accessed | tf_op | source)
XLA Modules:
  0.0 47.5 jit_solution(5446992760859461450)
XLA Ops:
  0.6 45.6 %place_and_attend.1 = (bf16[2,1,2,16,512]{4,3,2,1,0:T(8,128)(2,1)S(1)}, bf16[8,8,576]{2,1,0:T(8,128)(2,1)S(1)}) custom-call(bf16[8,64,576]{2,1,0:T(8,128)(2,1)} %prefill_hbm.1, s32[512]{0:T(512)} %stretch_hbm.1, s32[1,512]{1,0:T(1,128)} %bitcast.2, s32[2,512]{1,0:T(2,128)} %bitcast.3, s32[64,64]{1,0:T(8,128)} %plist_hbm.1, s32[64]{0:T(128)} %lengths_hbm.1, ...), custom_call_target="tpu_custom_call" | custom-call | tf_op jit(solution)/shard_map/place_and_attend/pallas_call | solution.py:403
  46.2 0.6 %copy.11 = bf16[2,1,2,16,512]{4,3,2,1,0:T(8,128)(2,1)} copy(bf16[2,1,2,16,512]{4,3,2,1,0:T(8,128)(2,1)S(1)} %get-tuple-element.4) | data formatting | bytes 131072
  46.8 0.6 %copy.12 = bf16[8,8,576]{2,1,0:T(8,128)(2,1)} copy(bf16[8,8,576]{2,1,0:T(8,128)(2,1)S(1)} %get-tuple-element.5) | data formatting | bytes 147456

commit v8 on v7

--- a/solution.py
+++ b/solution.py
@@ -141,8 +141,6 @@
 
     for copy in loads[3:]:
         copy.wait()
-    for i in depth_peers:
-        remote(all_queries.at[z], all_queries.at[z], q_send, q_recv, in_depth(i)).start()
     drain(incoming.at[pl.ds(0, 7)], s1_recv)
     arrived = incoming[...].astype(F32)
     whole = jnp.concatenate([arrived[:, 0:8, 0:256], arrived[:, 8:16, 0:256], arrived[:, 0:8, 256:384]], axis=2)
@@ -163,11 +161,11 @@
 
     def start_far(c):
         drain(gathered[c].at[0], s2_recv.at[c, 0])
+        along(c, 6, y - 2, (0, 32), 2)
         along(c, 4, y - 2, (0, 64), 1)
-        along(c, 6, y - 2, (0, 32), 2)
         drain(gathered[c].at[0], s2_recv.at[c, 1])
+        along(c, 7, y + 2, (32, 32), -2)
         along(c, 5, y + 2, (0, 64), -1)
-        along(c, 7, y + 2, (32, 32), -2)
 
     def part(ref, i, c):
         return ref[c].at[i]
@@ -220,6 +218,8 @@
         want = (first + 8 * (inner // 8)) * 8 + (inner & 7)
         picks[pl.ds(half * 256, 256), :] = hot(want == have_key)
 
+    for i in depth_peers:
+        remote(all_queries.at[z], all_queries.at[z], q_send, q_recv, in_depth(i)).start()
     for kind, c in ORDER[FIRST:]:
         start[kind](c)
 

time: 47.6 us -> 47.5 us (level)
  no operation moved by 1% of the time
where the time goes in v8:
time: 47.5 us; the launch traced here: 47.4 us
  Pallas kernels  45.5 us (96%)
  local copies, waits for them, and re-layouts  1.27 us (3%)
  between operations  0.64 us (1%)
    pallas_call x1, Pallas kernels, local(): pl.pallas_call(kernel, out_shape=(jax.ShapeDtypeStruct((2, 1, 2, 16, LAT)...  45.5 us
    unnamed x2, local copies, waits for them, and re-layouts  1.27 us

profile of v8, /device:TPU:1, one launch (start us, length us, event | category | flops | bytes accessed | tf_op | source)
XLA Modules:
  0.0 47.4 jit_solution(16060888341695073881)
XLA Ops:
  0.6 45.5 %place_and_attend.1 = (bf16[2,1,2,16,512]{4,3,2,1,0:T(8,128)(2,1)S(1)}, bf16[8,8,576]{2,1,0:T(8,128)(2,1)S(1)}) custom-call(bf16[8,64,576]{2,1,0:T(8,128)(2,1)} %prefill_hbm.1, s32[512]{0:T(512)} %stretch_hbm.1, s32[1,512]{1,0:T(1,128)} %bitcast.2, s32[2,512]{1,0:T(2,128)} %bitcast.3, s32[64,64]{1,0:T(8,128)} %plist_hbm.1, s32[64]{0:T(128)} %lengths_hbm.1, ...), custom_call_target="tpu_custom_call" | custom-call | tf_op jit(solution)/shard_map/place_and_attend/pallas_call | solution.py:403
  46.1 0.6 %copy.11 = bf16[2,1,2,16,512]{4,3,2,1,0:T(8,128)(2,1)} copy(bf16[2,1,2,16,512]{4,3,2,1,0:T(8,128)(2,1)S(1)} %get-tuple-element.4) | data formatting | bytes 131072
  46.7 0.6 %copy.12 = bf16[8,8,576]{2,1,0:T(8,128)(2,1)} copy(bf16[8,8,576]{2,1,0:T(8,128)(2,1)S(1)} %get-tuple-element.5) | data formatting | bytes 147456
